TPU v7x, 256 devices: a whole 4x4x8 slice. The times are simulated.
256 devices in a mesh: lon: 4 (over x), lat: 64 (over z, y, core).
Axes of the slice: x: 4, y: 4, z: 8, core: 2. Of those that a mesh axis runs over, the one named last changes fastest.
Arguments:
- tokens: bfloat16 [2, 384, 192, 512], P(None, 'lat', 'lon'), may hold values from -6 to 6
- qkv_weight: bfloat16 [512, 1536], replicated, may hold values from -0.25 to 0.25
- out_weight: bfloat16 [512, 512], replicated, may hold values from -0.25 to 0.25
- attn_gain: float32 [512], replicated, may hold values from 0.5 to 1.5
- logit_scale: float32 [8], replicated, may hold values from 4 to 16
- merge_weight: bfloat16 [2048, 1024], replicated, may hold values from -0.125 to 0.125
- merge_gain: float32 [2048], replicated, may hold values from 0.5 to 1.5
- split_weight: bfloat16 [1024, 2048], replicated, may hold values from -0.1875 to 0.1875
- split_gain: float32 [512], replicated, may hold values from 0.5 to 1.5
Outputs:
- decoded: bfloat16 [2, 384, 192, 512], P(None, 'lat', 'lon')
All inputs are finite; a program needn't handle non-finite values.
Results may differ from a plain program's by a relative error of at most 0.015.
Values may be sent and summed in bfloat16 or wider, within the bound.
No kernel may reach another device: no remote copies, remote signals or barrier semaphores. Data moves between devices by JAX's collectives and lax.ppermute only.
A program may use at most 128 MiB of HBM per device.

v0:
```python
import jax
import jax.numpy as jnp
from jax import lax
from jax.sharding import PartitionSpec as P


def passed_along(value, axis, steps):
    count = lax.axis_size(axis)
    pairs = [(source, (source + steps) % count) for source in range(count)]
    return lax.ppermute(value, axis, pairs)


def layer_norm(value, gain):
    value = value.astype(jnp.float32)
    centered = value - jnp.mean(value, -1, keepdims=True)
    variance = jnp.mean(centered * centered, -1, keepdims=True)
    return centered * lax.rsqrt(variance + 1e-05) * gain


def partition(array):
    depth, height, span, feats = array.shape
    shaped = array.reshape(depth // 2, 2, height // 6, 6, span // 12, 12, feats)
    shaped = shaped.transpose(0, 2, 4, 1, 3, 5, 6)
    return shaped.reshape(depth // 2 * (height // 6) * (span // 12), 144, feats)


def unpartition(array, depth, height, span):
    feats = array.shape[-1]
    shaped = array.reshape(depth // 2, height // 6, span // 12, 2, 6, 12, feats)
    shaped = shaped.transpose(0, 3, 1, 4, 2, 5, 6)
    return shaped.reshape(depth, height, span, feats)


def window_block(qwin, key_value_window, mwin, scales):
    token_count, window_cells, channel_width = qwin.shape
    head_count = scales.shape[0]
    window_size = channel_width // head_count
    qval = qwin.astype(jnp.float32).reshape(token_count, window_cells, head_count, window_size)
    kval = (
        key_value_window[:, :, :channel_width]
        .astype(jnp.float32)
        .reshape(token_count, window_cells, head_count, window_size)
    )
    value_vectors = key_value_window[:, :, channel_width:].reshape(
        token_count, window_cells, head_count, window_size
    )
    qnorm = qval * lax.rsqrt(jnp.sum(qval * qval, -1, keepdims=True) + 1e-06)
    knorm = kval * lax.rsqrt(jnp.sum(kval * kval, -1, keepdims=True) + 1e-06)
    scores = jnp.einsum("wqhd,wkhd->whqk", qnorm, knorm, precision=lax.Precision.HIGHEST)
    scores = scores * scales[None, :, None, None]
    expo = jnp.exp(scores) * mwin[:, None, :, :]
    softmax_weight = (expo / jnp.sum(expo, -1, keepdims=True)).astype(jnp.bfloat16)
    attended_output = jnp.einsum(
        "nxtm,nmxv->ntxv", softmax_weight, value_vectors, preferred_element_type=jnp.float32
    )
    return attended_output.astype(jnp.bfloat16).reshape(token_count, window_cells, channel_width)


def attend(query, keyval, mask, scales):
    depth, height, span, channel_width = query.shape
    groups = depth // 2
    qwin = partition(query)
    key_value_window = partition(keyval)
    token_count = qwin.shape[0]
    per = token_count // groups

    def one_group(item):
        return window_block(item[0], item[1], item[2], scales)

    result = lax.map(
        one_group,
        (
            qwin.reshape(groups, per, 144, channel_width),
            key_value_window.reshape(groups, per, 144, 2 * channel_width),
            mask.reshape((groups, per) + mask.shape[1:]),
        ),
    )
    return unpartition(result.reshape(token_count, 144, channel_width), depth, height, span)


def merge_split(skip, merge_weight, merge_gain, split_weight, split_gain):
    levels, rows, cols, channel_width = skip.shape
    blocks = skip.reshape(levels, rows // 2, 2, cols // 2, 2, channel_width).transpose(
        0, 1, 3, 4, 2, 5
    )
    merged = blocks.reshape(-1, 4 * channel_width)
    merged_normed = layer_norm(merged, merge_gain).astype(jnp.bfloat16)
    coarse = jnp.dot(merged_normed, merge_weight, preferred_element_type=jnp.float32).astype(
        jnp.bfloat16
    )
    expanded = jnp.dot(coarse, split_weight, preferred_element_type=jnp.float32)
    expanded = layer_norm(expanded.reshape(-1, 4, channel_width), split_gain)
    expanded = expanded.reshape(levels, rows // 2, cols // 2, 2, 2, channel_width).transpose(
        0, 1, 4, 2, 3, 5
    )
    expanded = expanded.reshape(levels, rows, cols, channel_width)
    return (skip.astype(jnp.float32) + expanded).astype(jnp.bfloat16)


def body(
    tokens,
    qkv_weight,
    out_weight,
    attn_gain,
    logit_scale,
    merge_weight,
    merge_gain,
    split_weight,
    split_gain,
):
    levels, rows, cols, channel_width = tokens.shape
    normed = layer_norm(tokens, attn_gain).astype(jnp.bfloat16)
    band_rows = rows * lax.axis_size("lat")
    edge = passed_along(normed[:, :, cols - 6 :], "lon", 1)
    turned = jnp.concatenate([edge, normed[:, :, : cols - 6]], 2)
    upper = passed_along(turned[:, rows - 3 :], "lat", 1)
    turned = jnp.concatenate([upper, turned[:, : rows - 3]], 1)
    turned = jnp.concatenate([turned[levels - 1 :], turned[: levels - 1]], 0)
    projected_all = jnp.dot(
        turned.reshape(-1, channel_width), qkv_weight, preferred_element_type=jnp.float32
    )
    projected_all = projected_all.astype(jnp.bfloat16).reshape(
        levels, rows, cols, 3 * channel_width
    )
    query = projected_all[..., :channel_width]
    keyval = projected_all[..., channel_width:]
    level_index = jnp.arange(levels, dtype=jnp.int32)
    level_label = ((level_index + levels - 1) % levels + 1) // 2
    row_global = (
        lax.axis_index("lat") * rows + jnp.arange(rows, dtype=jnp.int32) - 3 + band_rows
    ) % band_rows
    row_label = (row_global + 3) // 6
    label = level_label[:, None] * band_rows + row_label[None, :]
    label = jnp.broadcast_to(label[:, :, None, None], (levels, rows, cols, 1))
    label_win = partition(label)[:, :, 0]
    mask = (label_win[:, :, None] == label_win[:, None, :]).astype(jnp.float32)
    attended_output = attend(query, keyval, mask, logit_scale)
    attended_output = jnp.concatenate([attended_output[1:], attended_output[:1]], 0)
    lower = passed_along(attended_output[:, :3], "lat", -1)
    attended_output = jnp.concatenate([attended_output[:, 3:], lower], 1)
    right = passed_along(attended_output[:, :, :6], "lon", -1)
    attended_output = jnp.concatenate([attended_output[:, :, 6:], right], 2)
    projected = jnp.dot(
        attended_output.reshape(-1, channel_width), out_weight, preferred_element_type=jnp.float32
    )
    skip = (
        tokens.astype(jnp.float32) + projected.reshape(levels, rows, cols, channel_width)
    ).astype(jnp.bfloat16)
    return merge_split(skip, merge_weight, merge_gain, split_weight, split_gain)


def solution(mesh):
    placed = (P(None, "lat", "lon", None), P(), P(), P(), P(), P(), P(), P(), P())
    return jax.shard_map(
        body, mesh=mesh, in_specs=placed, out_specs=P(None, "lat", "lon", None), check_vma=False
    )
```

profile of v0, /device:TPU:127, one launch (start us, length us, event | category | flops | bytes accessed | tf_op | source)
XLA Modules:
  0.0 106.2 jit_solution(9768431572288459990)
XLA Ops:
  0.0 1.4 %convert_reduce_fusion = f32[2,6,48]{2,1,0:T(8,128)S(1)} fusion(bf16[2,6,48,512]{3,2,1,0:T(8,128)(2,1)} %param.9), kind=kLoop, calls=%fused_computation.12 | loop fusion | flops 589248 | bytes 592128 | tf_op jit(solution)/shard_map/reduce_sum | solution.py:15
  1.4 1.4 %fusion.11 = f32[2,6,48]{2,1,0:T(8,128)S(1)} fusion(bf16[2,6,48,512]{3,2,1,0:T(8,128)(2,1)} %param.9, f32[2,6,48]{2,1,0:T(8,128)S(1)} %broadcast_multiply_fusion.3), kind=kLoop, calls=%fused_computation.20 | loop fusion | flops 1179072 | bytes 594432 | tf_op jit(solution)/shard_map/reduce_sum | solution.py:16
  2.8 0.3 fusion.13
  3.1 0.3 collective-permute-start
  3.4 3.2 %collective-permute-done = bf16[2,6,6,512]{3,2,1,0:T(8,128)(2,1)S(1)} collective-permute-done((bf16[2,6,6,512]{3,2,1,0:T(8,128)(2,1)S(1)}, bf16[2,6,6,512]{3,2,1,0:T(8,128)(2,1)S(1)}, u32[]{:S(2)}, u32[]{:S(2)}) %collective-permute-start) | collective-permute-done | bytes 73760 | tf_op jit(solution)/shard_map/ppermute | solution.py:10
  6.7 4.5 %collective-permute-start.1 = (bf16[2,3,48,512]{3,2,1,0:T(8,128)(2,1)S(1)}, bf16[2,3,48,512]{3,2,1,0:T(8,128)(2,1)S(1)}, u32[]{:S(2)}, u32[]{:S(2)}) collective-permute-start(bf16[2,3,48,512]{3,2,1,0:T(8,128)(2,1)S(1)} %fusion.29), channel_id=1, source_target_pairs={{0,1},{1,2},{2,3},{3,4},{4,5},{5,6},{6,7},{7,8},{8,9},{9,10},{10,1... | collective-permute-start | bytes 884744 | tf_op jit(solution)/shard_map/ppermute | solution.py:10
  11.5 0.9 compare_convert_fusion
  12.4 2.5 %collective-permute-done.1 = bf16[2,3,48,512]{3,2,1,0:T(8,128)(2,1)S(1)} collective-permute-done((bf16[2,3,48,512]{3,2,1,0:T(8,128)(2,1)S(1)}, bf16[2,3,48,512]{3,2,1,0:T(8,128)(2,1)S(1)}, u32[]{:S(2)}, u32[]{:S(2)}) %collective-permute-start.1) | collective-permute-done | bytes 294944 | tf_op jit(solution)/shard_map/ppermute | solution.py:10
  15.1 1.1 %convolution_convert_fusion = bf16[576,1536]{1,0:T(8,128)(2,1)S(1)} fusion(bf16[576,512]{1,0:T(8,128)(2,1)S(1)} %bitcast.57, bf16[512,1536]{1,0:T(8,128)(2,1)S(1)} %copy-done), kind=kOutput, calls=%fused_computation.3 | convolution fusion | flops 906854400 | bytes 3932160 | tf_op jit(solution)/shard_map/dot_general | solution.py:119
  16.4 1.2 %slice_convert_fusion = f32[2,6,48,512]{3,2,1,0:T(8,128)} fusion(bf16[2,6,48,1536]{3,2,1,0:T(8,128)(2,1)S(1)} %bitcast.55), kind=kLoop, calls=%fused_computation.36 | loop fusion | flops 294912 | bytes 1769472 | tf_op jit(solution)/shard_map/while/body/eval_jaxpr/convert_element_type | solution.py:38
  17.5 1.2 %copy.115 = bf16[2,6,48,1024]{3,0,2,1:T(2,128)(2,1)S(1)} copy(bf16[2,6,48,1024]{3,2,1,0:T(8,128)(2,1)S(1)} %slice.80) | data formatting | bytes 2359296
  18.8 0.9 copy.91
  19.7 1.2 %fusion.36 = (bf16[4,144,512]{2,0,1:T(4,128)(2,1)S(1)}, bf16[4,144,512]{2,0,1:T(4,128)(2,1)}) fusion(bf16[4,144,1024]{2,0,1:T(4,128)(2,1)S(1)} %bitcast.50), kind=kLoop, calls=%fused_computation.79 | loop fusion | bytes 2359296 | tf_op jit(solution)/shard_map/while/body/eval_jaxpr/slice | solution.py:40
  21.1 1.9 %reshape.246 = f32[4,144,8,64]{3,2,1,0:T(8,128)} reshape(f32[4,144,512]{2,1,0:T(8,128)S(1)} %copy_convert_fusion) | data formatting | bytes 2359296 | tf_op jit(solution)/shard_map/while/body/eval_jaxpr/reshape | solution.py:42
  23.0 2.4 %multiply_reduce_fusion = f32[4,144,8]{2,1,0:T(8,128)S(1)} fusion(f32[4,144,8,64]{3,2,1,0:T(8,128)} %reshape.246), kind=kLoop, calls=%fused_computation.7 | loop fusion | flops 585216 | bytes 1198080 | tf_op jit(solution)/shard_map/while/body/eval_jaxpr/reduce_sum | solution.py:48
  25.3 0.2 copy.98
  25.7 3.2 %broadcast_multiply_fusion = f32[4,144,8,64]{3,2,1,0:T(8,128)} fusion(f32[4,144,8,64]{3,2,1,0:T(8,128)} %reshape.246, f32[4,144,8]{2,1,0:T(8,128)S(1)} %copy.99), kind=kLoop, calls=%fused_computation.32 | loop fusion | flops 294912 | bytes 2377728 | tf_op jit(solution)/shard_map/while/body/eval_jaxpr/mul | solution.py:48
  28.8 0.9 copy.118
  29.8 0.8 copy.94
  30.5 2.1 %reshape.244 = f32[4,144,8,64]{3,2,0,1:T(8,128)} reshape(f32[1,1,4,2,6,12,512]{6,2,5,4,3,1,0:T(4,128)S(1)} %copy.94) | data formatting | bytes 2359296 | tf_op jit(solution)/shard_map/while/body/eval_jaxpr/convert_element_type | solution.py:38
  32.7 2.4 %multiply_reduce_fusion.1 = f32[4,144,8]{2,0,1:T(4,128)S(1)} fusion(f32[4,144,8,64]{3,2,0,1:T(8,128)} %reshape.244), kind=kLoop, calls=%fused_computation.8 | loop fusion | flops 585216 | bytes 1198080 | tf_op jit(solution)/shard_map/while/body/eval_jaxpr/reduce_sum | solution.py:47
  35.3 0.2 copy.96
  35.5 3.1 %broadcast_multiply_fusion.1 = f32[4,144,8,64]{3,2,0,1:T(8,128)} fusion(f32[4,144,8,64]{3,2,0,1:T(8,128)} %reshape.244, f32[4,144,8]{2,0,1:T(4,128)S(1)} %copy.96), kind=kLoop, calls=%fused_computation.33 | loop fusion | flops 294912 | bytes 2377728 | tf_op jit(solution)/shard_map/while/body/eval_jaxpr/mul | solution.py:47
  38.6 1.4 %copy.92 = bf16[4,144,512]{1,2,0:T(8,128)(2,1)} copy(bf16[4,144,512]{2,0,1:T(4,128)(2,1)S(1)} %copy-done.5) | data formatting | bytes 1179648 | tf_op jit(solution)/shard_map/while/body/eval_jaxpr/slice | solution.py:44
  40.0 8.7 %fusion = (f32[4,8,144]{2,1,0:T(8,128)S(1)}, f32[4,8,144,144]{2,3,1,0:T(8,128)S(1)}) fusion(f32[4,144,144]{1,2,0:T(8,128)S(1)} %copy-done.4, f32[8]{0:T(128)S(1)} %copy-done.11, f32[4,144,8,64]{3,2,1,0:T(8,128)} %broadcast_multiply_fusion, f32[4,144,8,64]{3,2,0,1:T(8,128)} %broadcast_multiply_fusion.1), kind=kOutput, calls=%fused_computation.2 | convolution fusion | flops 511593984 | bytes 5363744 | tf_op jit(solution)/shard_map/while/body/eval_jaxpr/wqhd,wkhd->whqk/dot_general | solution.py:49
  48.8 2.3 %fusion.8 = bf16[4,144,8,64]{1,3,2,0:T(8,128)(2,1)} fusion(bf16[4,144,8,64]{1,3,2,0:T(8,128)(2,1)S(1)} %bitcast.56, f32[4,8,144,144]{2,3,1,0:T(8,128)S(1)} %get-tuple-element.32, f32[4,8,144]{2,1,0:T(8,128)S(1)} %get-tuple-element.31, f32[4,144,144]{1,2,0:T(8,128)S(1)} %copy-done.4, f32[8]{0:T(128)S(1)} %copy-done.11), kind=kOutput, calls=%fused_computation.16 | convolution fusion | flops 87883776 | bytes 4184096 | tf_op jit(solution)/shard_map/while/body/eval_jaxpr/nxtm,nmxv->ntxv/dot_general | solution.py:53
  51.1 2.1 %copy.103 = bf16[4,144,8,64]{3,2,0,1:T(8,128)(2,1)S(1)} copy(bf16[4,144,8,64]{1,3,2,0:T(8,128)(2,1)} %fusion.8) | data formatting | bytes 1179648 | tf_op jit(solution)/shard_map/while/body/eval_jaxpr/convert_element_type | solution.py:56
  53.2 1.5 %reshape_reshape.2 = bf16[1,1,4,2,6,12,512]{6,2,5,4,3,1,0:T(4,128)(2,1)} reshape(bf16[4,144,8,64]{3,2,0,1:T(8,128)(2,1)S(1)} %copy.103) | data formatting | bytes 1179648 | tf_op jit(solution)/shard_map/reshape;reshape | solution.py:29
  54.6 2.0 %fusion.38 = (bf16[1,1,1,6,4,12,512]{6,4,5,3,1,2,0:T(4,128)(2,1)}, bf16[1,1,1,6,4,12,512]{6,4,5,3,1,2,0:T(4,128)(2,1)S(1)}) fusion(bf16[1,2,1,6,4,12,512]{6,4,5,3,1,2,0:T(4,128)(2,1)} %bitcast.53), kind=kLoop, calls=%fused_computation.81 | loop fusion | bytes 1179648 | tf_op jit(solution)/shard_map/slice | solution.py:138
  56.8 1.0 copy.105
  58.0 0.2 collective-permute-start.2
  58.2 10.1 %collective-permute-done.2 = bf16[2,3,48,512]{3,2,1,0:T(8,128)(2,1)S(1)} collective-permute-done((bf16[2,3,48,512]{3,2,1,0:T(8,128)(2,1)S(1)}, bf16[2,3,48,512]{3,2,1,0:T(8,128)(2,1)S(1)}, u32[]{:S(2)}, u32[]{:S(2)}) %collective-permute-start.2) | collective-permute-done | bytes 294944 | tf_op jit(solution)/shard_map/ppermute | solution.py:10
  68.3 0.6 collective-permute-start.3
  69.1 4.0 %collective-permute-done.3 = bf16[2,6,6,512]{3,2,1,0:T(8,128)(2,1)S(1)} collective-permute-done((bf16[2,6,6,512]{3,2,1,0:T(8,128)(2,1)S(1)}, bf16[2,6,6,512]{3,2,1,0:T(8,128)(2,1)S(1)}, u32[]{:S(2)}, u32[]{:S(2)}) %collective-permute-start.3) | collective-permute-done | bytes 73760 | tf_op jit(solution)/shard_map/ppermute | solution.py:10
  73.1 1.5 %fusion.10 = f32[2,6,48,512]{3,2,1,0:T(8,128)} fusion(bf16[2,6,48,512]{3,2,1,0:T(8,128)(2,1)S(1)} %copy-done.2, bf16[2,6,6,512]{3,2,1,0:T(8,128)(2,1)S(1)} %collective-permute-done.3, bf16[2,6,42,512]{3,2,1,0:T(8,128)(2,1)S(1)} %slice_maximum_fusion, bf16[512,512]{1,0:T(8,128)(2,1)S(1)} %copy-done.7), kind=kOutput, calls=%fused_computation.18 | convolution fusion | flops 304349184 | bytes 2883584 | tf_op jit(solution)/shard_map/dot_general | solution.py:143
  74.6 2.0 %reshape.250 = f32[2,3,2,24,2,512]{5,4,3,2,1,0:T(2,128)S(1)} reshape(f32[2,6,48,512]{3,2,1,0:T(8,128)} %fusion.10) | data formatting | bytes 2359296 | tf_op jit(solution)/shard_map/convert_element_type | solution.py:14
  76.6 1.1 fusion.35
  77.6 2.0 %copy.142 = f32[2,3,2,24,2,512]{5,2,4,3,1,0:T(2,128)} copy(f32[2,3,2,24,2,512]{5,4,3,2,1,0:T(2,128)S(1)} %reshape.250) | data formatting | bytes 2359296 | tf_op jit(solution)/shard_map/convert_element_type | solution.py:14
  79.6 1.3 %multiply_reduce_fusion.3 = f32[2,3,24]{2,1,0:T(4,128)S(1)} fusion(f32[2,3,24]{2,1,0:T(4,128)S(1)} %broadcast_multiply_fusion.4, f32[2,3,2,24,2,512]{5,4,3,2,1,0:T(2,128)S(1)} %reshape.250), kind=kLoop, calls=%fused_computation.31 | loop fusion | flops 884592 | bytes 1180800 | tf_op jit(solution)/shard_map/reduce_sum | solution.py:16
  81.0 3.2 %reshape.247 = f32[144,2048]{1,0:T(8,128)} reshape(f32[2,3,24,2,2,512]{5,4,3,2,1,0:T(2,128)} %bitcast.49) | data formatting | bytes 2359296 | tf_op jit(solution)/shard_map/convert_element_type | solution.py:14
  84.2 5.2 %fusion.17 = f32[144,2048]{1,0:T(8,128)S(1)} fusion(bf16[1024,2048]{1,0:T(8,128)(2,1)} %param.16, bf16[2048,1024]{1,0:T(8,128)(2,1)} %param.14, f32[144,2048]{1,0:T(8,128)} %reshape.247, f32[2048]{0:T(1024)S(1)} %copy-done.8, f32[144]{0:T(256)S(1)} %rsqrt.52, f32[144]{0:T(256)S(1)} %div.63), kind=kOutput, calls=%fused_computation.34 | convolution fusion | flops 1209286656 | bytes 10757248 | tf_op jit(solution)/shard_map/dot_general | solution.py:91
  89.5 1.8 %reshape.242 = f32[144,4,512]{2,1,0:T(4,128)} reshape(f32[144,2048]{1,0:T(8,128)S(1)} %fusion.17) | data formatting | bytes 2359296 | tf_op jit(solution)/shard_map/reshape | solution.py:92
  91.3 1.5 %reduce_sum.91 = f32[144,4]{1,0:T(8,128)S(1)} reduce(f32[144,4,512]{2,1,0:T(4,128)} %reshape.242, f32[]{:T(128)} %constant.82.clone.1), dimensions={2}, to_apply=%region_7.8 | reduce | flops 294336 | bytes 1181956 | tf_op jit(solution)/shard_map/reduce_sum | solution.py:15
  92.9 1.8 %multiply_reduce_fusion.2 = f32[144,4]{1,0:T(8,128)S(1)} fusion(f32[144,4,512]{2,1,0:T(4,128)} %reshape.242, f32[144,4]{1,0:T(8,128)S(1)} %broadcast_multiply_fusion.2), kind=kLoop, calls=%fused_computation.29 | loop fusion | flops 884160 | bytes 1184256 | tf_op jit(solution)/shard_map/reduce_sum | solution.py:16
  94.7 2.0 %reshape.241 = f32[2,3,24,2,2,512]{5,4,3,2,1,0:T(2,128)} reshape(f32[144,2048]{1,0:T(8,128)S(1)} %fusion.17) | data formatting | bytes 2359296 | tf_op jit(solution)/shard_map/reshape | solution.py:92
  97.4 3.5 %fusion.16 = f32[2,3,2,24,2,512]{5,4,3,2,1,0:T(2,128)} fusion(f32[2,3,24,2,2,512]{5,4,3,2,1,0:T(2,128)} %reshape.241, f32[512]{0:T(512)S(1)} %copy-done.10, f32[2,3,24,2,2]{3,2,4,1,0:T(8,128)S(1)} %copy.112, f32[2,3,24,2,2]{3,2,4,1,0:T(8,128)S(1)} %copy.108), kind=kLoop, calls=%fused_computation.26 | loop fusion | flops 884736 | bytes 2365952 | tf_op jit(solution)/shard_map/transpose | solution.py:93
  100.8 3.1 %reshape.243 = f32[2,6,48,512]{3,2,1,0:T(8,128)} reshape(f32[2,3,2,24,2,512]{5,4,3,2,1,0:T(2,128)} %fusion.16) | data formatting | bytes 2359296 | tf_op jit(solution)/shard_map/reshape | solution.py:96
  103.9 2.3 %add_convert_fusion = bf16[2,6,48,512]{3,2,1,0:T(8,128)(2,1)} fusion(f32[2,6,48,512]{3,2,1,0:T(8,128)S(1)} %copy-done.1, f32[2,6,48,512]{3,2,1,0:T(8,128)} %reshape.243), kind=kLoop, calls=%fused_computation.28 | loop fusion | flops 589824 | bytes 2949120 | tf_op jit(solution)/shard_map/convert_element_type | solution.py:97
  (62 shorter events, 2.6 us)
Async XLA Ops:
  0.0 15.1 %copy-start = (bf16[512,1536]{1,0:T(8,128)(2,1)S(1)}, bf16[512,1536]{1,0:T(8,128)(2,1)}, u32[]{:S(2)}) copy-start(bf16[512,1536]{1,0:T(8,128)(2,1)} %param.10) | copy-start | bytes 4718596
  0.0 2.8 %copy-start.2 = (bf16[2,6,48,512]{3,2,1,0:T(8,128)(2,1)S(1)}, bf16[2,6,48,512]{3,2,1,0:T(8,128)(2,1)}, u32[]{:S(2)}) copy-start(bf16[2,6,48,512]{3,2,1,0:T(8,128)(2,1)} %param.9) | copy-start | bytes 1769476
  0.0 2.8 %copy-start.9 = (f32[512]{0:T(512)S(1)}, f32[512]{0:T(512)}, u32[]{:S(2)}) copy-start(f32[512]{0:T(512)} %param.12) | copy-start | bytes 6148
  3.1 3.5 %collective-permute-start = (bf16[2,6,6,512]{3,2,1,0:T(8,128)(2,1)S(1)}, bf16[2,6,6,512]{3,2,1,0:T(8,128)(2,1)S(1)}, u32[]{:S(2)}, u32[]{:S(2)}) collective-permute-start(bf16[2,6,6,512]{3,2,1,0:T(8,128)(2,1)S(1)} %slice.74), channel_id=1, source_target_pairs={{0,64},{64,128},{128,192},{192,0},{1,65},{65,129},{129,193},{193,1... | collective-permute-start | bytes 221192 | tf_op jit(solution)/shard_map/ppermute | solution.py:10
  6.7 8.1 %collective-permute-start.1 = (bf16[2,3,48,512]{3,2,1,0:T(8,128)(2,1)S(1)}, bf16[2,3,48,512]{3,2,1,0:T(8,128)(2,1)S(1)}, u32[]{:S(2)}, u32[]{:S(2)}) collective-permute-start(bf16[2,3,48,512]{3,2,1,0:T(8,128)(2,1)S(1)} %fusion.29), channel_id=1, source_target_pairs={{0,1},{1,2},{2,3},{3,4},{4,5},{5,6},{6,7},{7,8},{8,9},{9,10},{10,1... | collective-permute-start | bytes 884744 | tf_op jit(solution)/shard_map/ppermute | solution.py:10
  25.7 3.2 %copy-start.3 = (f32[2,6,48,512]{3,2,1,0:T(8,128)S(1)}, f32[2,6,48,512]{3,2,1,0:T(8,128)}, u32[]{:S(2)}) copy-start(f32[2,6,48,512]{3,2,1,0:T(8,128)} %slice_convert_fusion) | copy-start | bytes 3538948
  35.5 3.1 %copy-start.5 = (bf16[4,144,512]{2,0,1:T(4,128)(2,1)S(1)}, bf16[4,144,512]{2,0,1:T(4,128)(2,1)}, u32[]{:S(2)}) copy-start(bf16[4,144,512]{2,0,1:T(4,128)(2,1)} %get-tuple-element.16) | copy-start | bytes 1769476
  38.6 1.4 %copy-start.4 = (f32[4,144,144]{1,2,0:T(8,128)S(1)}, f32[4,144,144]{1,2,0:T(8,128)}, u32[]{:S(2)}) copy-start(f32[4,144,144]{1,2,0:T(8,128)} %compare_convert_fusion) | copy-start | bytes 995332
  38.6 1.5 %copy-start.11 = (f32[8]{0:T(128)S(1)}, f32[8]{0:T(128)}, u32[]{:S(2)}) copy-start(f32[8]{0:T(128)} %param.13) | copy-start | bytes 100
  40.0 8.8 %copy-start.6 = (bf16[4,144,512]{1,2,0:T(8,128)(2,1)S(1)}, bf16[4,144,512]{1,2,0:T(8,128)(2,1)}, u32[]{:S(2)}) copy-start(bf16[4,144,512]{1,2,0:T(8,128)(2,1)} %copy.92) | copy-start | bytes 1769476
  58.0 15.1 %copy-start.7 = (bf16[512,512]{1,0:T(8,128)(2,1)S(1)}, bf16[512,512]{1,0:T(8,128)(2,1)}, u32[]{:S(2)}) copy-start(bf16[512,512]{1,0:T(8,128)(2,1)} %param.11) | copy-start | bytes 1572868
  58.0 10.3 %collective-permute-start.2 = (bf16[2,3,48,512]{3,2,1,0:T(8,128)(2,1)S(1)}, bf16[2,3,48,512]{3,2,1,0:T(8,128)(2,1)S(1)}, u32[]{:S(2)}, u32[]{:S(2)}) collective-permute-start(bf16[2,3,48,512]{3,2,1,0:T(8,128)(2,1)S(1)} %get-tuple-element.24), channel_id=1, source_target_pairs={{0,63},{1,0},{2,1},{3,2},{4,3},{5,4},{6,5},{7,6},{8,7},{9,8},{10,9... | collective-permute-start | bytes 884744 | tf_op jit(solution)/shard_map/ppermute | solution.py:10
  68.3 4.8 %collective-permute-start.3 = (bf16[2,6,6,512]{3,2,1,0:T(8,128)(2,1)S(1)}, bf16[2,6,6,512]{3,2,1,0:T(8,128)(2,1)S(1)}, u32[]{:S(2)}, u32[]{:S(2)}) collective-permute-start(bf16[2,6,6,512]{3,2,1,0:T(8,128)(2,1)S(1)} %pad_maximum_fusion.2), channel_id=1, source_target_pairs={{0,192},{64,0},{128,64},{192,128},{1,193},{65,1},{129,65},{193,129... | collective-permute-start | bytes 221192 | tf_op jit(solution)/shard_map/ppermute | solution.py:10
  81.0 3.2 %copy-start.8 = (f32[2048]{0:T(1024)S(1)}, f32[2048]{0:T(1024)}, u32[]{:S(2)}) copy-start(f32[2048]{0:T(1024)} %param.15) | copy-start | bytes 24580
  94.7 2.6 %copy-start.10 = (f32[512]{0:T(512)S(1)}, f32[512]{0:T(512)}, u32[]{:S(2)}) copy-start(f32[512]{0:T(512)} %param.17) | copy-start | bytes 6148
  100.8 3.1 %copy-start.1 = (f32[2,6,48,512]{3,2,1,0:T(8,128)S(1)}, f32[2,6,48,512]{3,2,1,0:T(8,128)}, u32[]{:S(2)}) copy-start(f32[2,6,48,512]{3,2,1,0:T(8,128)} %fusion.10) | copy-start | bytes 3538948
where the time goes:
time: 107 us; the launch traced here: 106 us
  local copies, waits for them, and re-layouts  33.3 us (31%)
  other arithmetic  28.3 us (26%)
  waiting for transfers between devices  19.8 us (19%)
  matrix products  18.8 us (18%)
  starting transfers between devices  5.54 us (5%)
    ppermute x4, waiting for transfers between devices, passed_along(): return lax.ppermute(value, axis, pairs)  19.8 us
    dot_general x1, matrix products, window_block(): jnp.einsum('wqhd,wkhd->whqk', qnorm, knorm, precision=lax.Precision.HIGHEST)  8.75 us
    convert_element_type x3, local copies, waits for them, and re-layouts, layer_norm(): value = value.astype(jnp.float32)  7.13 us
    ppermute x4, starting transfers between devices, passed_along(): return lax.ppermute(value, axis, pairs)  5.54 us
    dot_general x1, matrix products, merge_split(): expanded = jnp.dot(coarse, split_weight, preferred_element_type=jnp.float32)  5.25 us
    reduce_sum x3, other arithmetic, layer_norm(): variance = jnp.mean(centered * centered, -1, keepdims=True)  4.41 us
    reduce_sum x3, other arithmetic, layer_norm(): centered = value - jnp.mean(value, -1, keepdims=True)  3.93 us
    reshape x2, local copies, waits for them, and re-layouts, merge_split(): expanded = layer_norm(expanded.reshape(-1, 4, channel_width), split_gain)  3.88 us
  transfers between devices with their start and end apart: 4, of which 4 were waited for; matrix products, arithmetic and copies ran while one was open for 1% of the time, Pallas kernels for 0%

commit v1 on v0

v1 whole, which is shorter than its diff:
```python
import jax
import jax.numpy as jnp
from jax import lax
from jax.experimental import pallas as pl
from jax.experimental.pallas import tpu as pltpu
from jax.sharding import PartitionSpec as P

BF = jnp.bfloat16
F32 = jnp.float32
D = 512
LOG2E = 1.4426950408889634
VMEM = pl.BlockSpec(memory_space=pltpu.VMEM)
PARAMS = pltpu.CompilerParams(vmem_limit_bytes=24 * 2**20)


def dot(a, b):
    return jnp.dot(a, b, preferred_element_type=F32)


def dot_t(a, b):
    return lax.dot_general(a, b, (((1,), (1,)), ((), ())), preferred_element_type=F32)


def layer_norm(value, gain):
    centered = value - jnp.mean(value, -1, keepdims=True)
    variance = jnp.mean(centered * centered, -1, keepdims=True)
    return centered * lax.rsqrt(variance + 1e-05) * gain


def head_scaled(value, block, extra):
    rounded = value.astype(BF)
    squares = rounded * rounded
    sums = jnp.concatenate([dot(squares[:, :256], block), dot(squares[:, 256:], block)], 1)
    return value * (lax.rsqrt(sums + 1e-06) * extra)


def stack_heads(q):
    lane = lax.broadcasted_iota(jnp.int32, q.shape, 1)
    return jnp.concatenate(
        [jnp.where((lane >= 64 * h) & (lane < 64 * h + 64), q, 0.0) for h in range(4)], 0
    ).astype(BF)


def unstack_heads(value, m, split):
    lane = lax.broadcasted_iota(jnp.int32, (m, 128), 1)
    halves = []
    for g in range(2):
        col = slice(128 * g, 128 * g + 128) if split else slice(0, 128)
        first = value[2 * g * m : (2 * g + 1) * m, col]
        second = value[(2 * g + 1) * m : (2 * g + 2) * m, col]
        halves.append(jnp.where(lane < 64, first, second))
    return jnp.concatenate(halves, 1)


def scores_to_sums(q, k, v, mask, ones, heads):
    m = q.shape[0]
    inverse = lax.rsqrt(dot_t(heads, k * k) + 1e-06)
    scores = dot_t(stack_heads(q), k)
    weight = [jnp.exp2(scores[m * h : m * h + m] * inverse[h : h + 1]) for h in range(4)]
    weight = jnp.concatenate(weight, 0).astype(BF) * mask
    return (
        unstack_heads(dot(weight, v), m, True),
        unstack_heads(dot(weight, ones), m, False),
    )


def head_rows():
    row = lax.broadcasted_iota(jnp.int32, (16, 256), 0)
    lane = lax.broadcasted_iota(jnp.int32, (16, 256), 1)
    return jnp.where(row == lax.shift_right_logical(lane, 6), 1.0, 0.0).astype(BF)


def window(col):
    return lax.shift_right_logical((col + 18) * 5462, 16)


def present_rows():
    lat = lax.axis_index("lat")
    return jnp.where((lat > 0) & (lat < lax.axis_size("lat") - 1), 1.0, 0.0)


def main_mask(ch, present):
    query = lax.broadcasted_iota(jnp.int32, (72, 192), 0)
    key = lax.broadcasted_iota(jnp.int32, (72, 192), 1)
    row = (query >= 24).astype(jnp.int32) + (query >= 48).astype(jnp.int32)
    same = window(24 * ch + query - 24 * row) == window(16 * ch + (key & 31))
    value = jnp.where(same, jnp.where(key < 96, 1.0, present), 0.0)
    return jnp.concatenate([value] * 4, 0).astype(BF)


def edge_mask(side, present):
    query = lax.broadcasted_iota(jnp.int32, (96, 192), 0)
    key = lax.broadcasted_iota(jnp.int32, (96, 192), 1)
    same = window(40 * side + (query & 7)) == window((48 if side else -8) + (key & 7))
    value = jnp.zeros((96, 192), F32)
    for group in range(4):
        rows = (query >= 24 * group) & (query < 24 * group + 24)
        keys = (key >= 48 * group) & (key < 48 * group + 48)
        other = present if group % 2 == 0 else 1.0
        value = jnp.where(rows & keys & same, jnp.where(key < 48 * group + 24, 1.0, other), value)
    return jnp.concatenate([value] * 4, 0).astype(BF)


def head_blocks():
    row = lax.broadcasted_iota(jnp.int32, (256, 256), 0)
    lane = lax.broadcasted_iota(jnp.int32, (256, 256), 1)
    same = lax.shift_right_logical(row, 6) == lax.shift_right_logical(lane, 6)
    return jnp.where(same, 1.0, 0.0).astype(BF)


def attend_half(q, kown, vown, kpart, vpart, present, osum, wsum):
    ones = jnp.ones((192, 128), BF)
    heads = head_rows()
    for ch in range(2):
        mask = main_mask(ch, present)
        for lv in range(2):
            qs = jnp.concatenate([q[lv, r, 24 * ch : 24 * ch + 24] for r in range(3)], 0)
            cells = slice(16 * ch, 16 * ch + 32)
            for hg in range(2):
                feats = slice(256 * hg, 256 * hg + 256)
                k = jnp.concatenate([x[lv, r, cells, feats] for x in (kown, kpart) for r in range(3)], 0)
                v = jnp.concatenate([x[lv, r, cells, feats] for x in (vown, vpart) for r in range(3)], 0)
                o, w = scores_to_sums(qs[:, feats], k, v, mask, ones, heads)
                for r in range(3):
                    osum[lv, r, 24 * ch : 24 * ch + 24, feats] = o[24 * r : 24 * r + 24]
                    wsum[lv, r, 24 * ch : 24 * ch + 24, feats] = w[24 * r : 24 * r + 24]


def project(x_ref, lv, gain, weight, columns):
    normed = layer_norm(x_ref[lv].reshape(144, D).astype(F32), gain).astype(BF)
    return dot(normed, weight[:, columns])


def rows_kernel(tokens, near, far):
    start = 3 * lax.rem(lax.axis_index("lat"), 2)
    near[...] = tokens[:, pl.ds(3 - start, 3)]
    far[...] = tokens[:, pl.ds(start, 3)]


def own_kernel(
    xj, xi, ri, weight, gain, scales, qj, qi, kj, vj, osum, wsum, ki, vi, kr, vr
):
    block = head_blocks()
    lane = lax.broadcasted_iota(jnp.int32, (1, D), 1)
    scale = jnp.zeros((1, D), F32)
    for h in range(8):
        scale = jnp.where(lax.shift_right_logical(lane, 6) == h, scales[:, h : h + 1], scale)
    scale = scale * LOG2E
    for lv in range(2):
        for x, q, k, v in ((xi, qi, ki, vi), (xj, qj, kj, vj)):
            all3 = project(x, lv, gain[...], weight, slice(0, 1536))
            q[lv] = head_scaled(all3[:, :D], block, scale).reshape(3, 48, D)
            k[lv] = all3[:, D : 2 * D].astype(BF).reshape(3, 48, D)
            v[lv] = all3[:, 2 * D :].astype(BF).reshape(3, 48, D)
        both = project(ri, lv, gain[...], weight, slice(512, 1536))
        kr[lv] = both[:, :D].astype(BF).reshape(3, 48, D)
        vr[lv] = both[:, D:].astype(BF).reshape(3, 48, D)
    attend_half(qi, ki, vi, kr, vr, 1.0, osum, wsum)


def far_kernel(rj, weight, gain, qj, kj, vj, osum, wsum, kr, vr):
    for lv in range(2):
        both = project(rj, lv, gain[...], weight, slice(512, 1536))
        kr[lv] = both[:, :D].astype(BF).reshape(3, 48, D)
        vr[lv] = both[:, D:].astype(BF).reshape(3, 48, D)
    attend_half(qj, kj, vj, kr, vr, present_rows(), osum, wsum)


def last_kernel(
    left, right, xj, xi, qj, qi, oj, wj, oi, wi, qkv, gain,
    out_weight, merge_weight, merge_gain, split_weight, split_gain, out,
    attended, skip, fine,
):
    ones128 = jnp.ones((192, 128), BF)
    heads = head_rows()
    tops = (qj, qi)
    sums = ((oj, wj), (oi, wi))
    for half, (o, w) in enumerate(sums):
        attended[half, :, :, 8:40] = o[:, :, 8:40] * pl.reciprocal(w[:, :, 8:40], approx=True)
    for side, x in enumerate((left, right)):
        normed = layer_norm(x[...].astype(F32), gain[...]).astype(BF)
        both = dot(normed, qkv[:, D:])
        k = both[:, :D].astype(BF)
        v = both[:, D:].astype(BF)
        near = slice(40 * side, 40 * side + 8)
        q = jnp.concatenate(
            [tops[half][lv, r, near] for lv in range(2) for half in range(2) for r in range(3)], 0
        )
        sel = edge_mask(side, present_rows())
        for hg in range(2):
            feats = slice(256 * hg, 256 * hg + 256)
            oe, we = scores_to_sums(q[:, feats], k[:, feats], v[:, feats], sel, ones128, heads)
            at = 0
            for lv in range(2):
                for half, (o, w) in enumerate(sums):
                    for r in range(3):
                        whole = w[lv, r, near, feats] + we[at : at + 8]
                        part = o[lv, r, near, feats] + oe[at : at + 8]
                        attended[half, lv, r, near, feats] = part * pl.reciprocal(whole, approx=True)
                        at += 8
    for half, x in enumerate((xj, xi)):
        value = dot(attended[half].reshape(288, D).astype(BF), out_weight[...])
        value = x[...].reshape(288, D).astype(F32) + value
        value = value.astype(BF).astype(F32).reshape(2, 3, 48, D)
        for f in range(4):
            skip[half, :, :, f] = value[..., 128 * f : 128 * f + 128]
    parity = lax.rem(lax.axis_index("lat"), 2)
    groups = []
    for c in range(2):
        for r in range(2):
            pieces = []
            for lv in range(2):
                for a in range(3):
                    row = 2 * a + r
                    half = parity if row < 3 else 1 - parity
                    chunks = [skip[half, lv, row % 3, f, pl.ds(c, 24, stride=2), :] for f in range(4)]
                    pieces.append(jnp.concatenate(chunks, 1))
            groups.append(jnp.concatenate(pieces, 0))
    mean = sum(jnp.sum(g, -1, keepdims=True) for g in groups) * (1.0 / 2048)
    centered = [g - mean for g in groups]
    variance = sum(jnp.sum(g * g, -1, keepdims=True) for g in centered) * (1.0 / 2048)
    inverse = lax.rsqrt(variance + 1e-05)
    merged = jnp.concatenate(
        [
            (g * inverse * merge_gain[:, D * i : D * i + D]).astype(BF)
            for i, g in enumerate(centered)
        ],
        1,
    )
    coarse = dot(merged, merge_weight[...]).astype(BF)
    for c in range(2):
        for r in range(2):
            i = 2 * c + r
            expanded = dot(coarse, split_weight[:, D * i : D * i + D])
            done = groups[i] + layer_norm(expanded, split_gain[...])
            for lv in range(2):
                for a in range(3):
                    at = (lv * 3 + a) * 24
                    for f in range(4):
                        fine[lv, 2 * a + r, f, pl.ds(c, 24, stride=2), :] = done[
                            at : at + 24, 128 * f : 128 * f + 128
                        ]
    for f in range(4):
        out[:, :, :, 128 * f : 128 * f + 128] = fine[:, :, f].astype(BF)


def body(
    tokens,
    qkv_weight,
    out_weight,
    attn_gain,
    logit_scale,
    merge_weight,
    merge_gain,
    split_weight,
    split_gain,
):
    lats = lax.axis_size("lat")
    pair = [(i, i ^ 1) for i in range(lats)]
    cross = [(i, ((i + 1) ^ 1) - 1) for i in range(1, lats - 1)]

    def along(value, steps):
        count = lax.axis_size("lon")
        return lax.ppermute(value, "lon", [(i, (i + steps) % count) for i in range(count)])

    def cells(dtype):
        return jax.ShapeDtypeStruct((2, 3, 48, D), dtype)

    xi, xj = pl.pallas_call(
        rows_kernel,
        name="rows",
        out_shape=[cells(BF), cells(BF)],
        in_specs=[VMEM],
        out_specs=[VMEM] * 2,
        compiler_params=PARAMS,
        cost_estimate=pl.CostEstimate(flops=5 * 10**9, bytes_accessed=10**6, transcendentals=0),
    )(tokens)
    ri = lax.ppermute(xi, "lat", pair)
    rj_edge = lax.ppermute(jnp.concatenate([xj[:, :, :8], xj[:, :, 40:]], 2), "lat", cross)
    rj_mid = lax.ppermute(xj[:, :, 8:40], "lat", cross)

    def edge_cells(own, far):
        parts = [xj[:, :, own], rj_edge[:, :, far], xi[:, :, own], ri[:, :, own]]
        return jnp.concatenate(parts, 1).reshape(192, D)

    to_left = edge_cells(slice(0, 8), slice(0, 8))
    to_right = edge_cells(slice(40, 48), slice(8, 16))
    to_left, to_right, ri = lax.optimization_barrier((to_left, to_right, ri))
    left = along(to_right, 1)
    right = along(to_left, -1)

    gain = attn_gain.reshape(1, D)

    scratch = [pltpu.VMEM((2, 3, 48, D), BF)]
    qj, qi, kj, vj, oi, wi = pl.pallas_call(
        own_kernel,
        name="own_cells",
        out_shape=[cells(F32), cells(F32), cells(BF), cells(BF), cells(F32), cells(F32)],
        in_specs=[VMEM] * 6,
        out_specs=[VMEM] * 6,
        scratch_shapes=scratch * 4,
        compiler_params=PARAMS,
        cost_estimate=pl.CostEstimate(flops=3 * 10**9, bytes_accessed=4 * 10**6, transcendentals=10**6),
    )(xj, xi, ri, qkv_weight, gain, logit_scale.reshape(1, 8))
    rj_mid, qj = lax.optimization_barrier((rj_mid, qj))
    rj = jnp.concatenate([rj_edge[:, :, :8], rj_mid, rj_edge[:, :, 8:]], 2)
    oj, wj = pl.pallas_call(
        far_kernel,
        name="far_rows",
        out_shape=[cells(F32), cells(F32)],
        in_specs=[VMEM] * 6,
        out_specs=[VMEM] * 2,
        scratch_shapes=scratch * 2,
        compiler_params=PARAMS,
        cost_estimate=pl.CostEstimate(flops=2 * 10**9, bytes_accessed=4 * 10**6, transcendentals=10**6),
    )(rj, qkv_weight, gain, qj, kj, vj)
    return pl.pallas_call(
        last_kernel,
        name="edges_merge_split",
        out_shape=jax.ShapeDtypeStruct((2, 6, 48, D), BF),
        in_specs=[VMEM] * 17,
        out_specs=VMEM,
        scratch_shapes=[
            pltpu.VMEM((2, 2, 3, 48, D), F32),
            pltpu.VMEM((2, 2, 3, 4, 48, 128), F32),
            pltpu.VMEM((2, 6, 4, 48, 128), F32),
        ],
        compiler_params=PARAMS,
        cost_estimate=pl.CostEstimate(flops=3 * 10**9, bytes_accessed=12 * 10**6, transcendentals=10**6),
    )(
        left, right, xj, xi, qj, qi, oj, wj, oi, wi, qkv_weight, gain,
        out_weight, merge_weight, merge_gain.reshape(1, 4 * D), split_weight, split_gain.reshape(1, D),
    )


def solution(mesh):
    placed = (P(None, "lat", "lon", None), P(), P(), P(), P(), P(), P(), P(), P())
    return jax.shard_map(
        body, mesh=mesh, in_specs=placed, out_specs=P(None, "lat", "lon", None), check_vma=False
    )
```

time: 107 us -> 27.9 us (0.26)
  the two profiles are of different devices: /device:TPU:127 before, /device:TPU:128 now
where the time goes in v1:
time: 27.9 us; the launch traced here: 27.8 us
  Pallas kernels  12.4 us (44%)
  starting transfers between devices  12.3 us (44%)
  waiting for transfers between devices  1.55 us (6%)
  local copies, waits for them, and re-layouts  1.27 us (5%)
    pallas_call x1, Pallas kernels, body(): pl.pallas_call(last_kernel, name='edges_merge_split', out_shape=jax.Shape...  5.27 us
    ppermute x1, starting transfers between devices, body(): rj_mid = lax.ppermute(xj[:, :, 8:40], 'lat', cross)  4.98 us
    pallas_call x1, Pallas kernels, body(): pl.pallas_call(own_kernel, name='own_cells', out_shape=[cells(F32), cells...  4.2 us
    ppermute x1, starting transfers between devices, body(): lax.ppermute(jnp.concatenate([xj[:, :, :8], xj[:, :, 40:]], 2), 'lat', cr...  3.91 us
    ppermute x2, starting transfers between devices, along(): lax.ppermute(value, 'lon', [(i, (i + steps) % count) for i in range(count)])  3.31 us
    pallas_call x1, Pallas kernels, body(): pl.pallas_call(far_kernel, name='far_rows', out_shape=[cells(F32), cells(...  2.86 us
    ppermute x1, waiting for transfers between devices, body(): ri = lax.ppermute(xi, 'lat', pair)  1.32 us
    unnamed x18, local copies, waits for them, and re-layouts  1.22 us
  transfers between devices with their start and end apart: 5, of which 2 were waited for; matrix products, arithmetic and copies ran while one was open for 0% of the time, Pallas kernels for 25%

profile of v1, /device:TPU:128, one launch (start us, length us, event | category | flops | bytes accessed | tf_op | source)
XLA Modules:
  0.0 27.8 jit_solution(6254162697960083456)
XLA Ops:
  0.0 0.0 copy-start.2
  0.0 0.0 copy-start.5
  0.0 0.0 copy-start.7
  0.0 1.2 %copy-done.7 = bf16[2,6,48,512]{3,2,1,0:T(8,128)(2,1)S(1)} copy-done((bf16[2,6,48,512]{3,2,1,0:T(8,128)(2,1)S(1)}, bf16[2,6,48,512]{3,2,1,0:T(8,128)(2,1)}, u32[]{:S(2)}) %copy-start.7) | copy-done | bytes 589848
  1.2 0.0 copy-start.8
  1.3 3.9 %collective-permute-start = (bf16[2,3,16,512]{3,2,1,0:T(8,128)(2,1)S(1)}, bf16[2,3,16,512]{3,2,1,0:T(8,128)(2,1)S(1)}, u32[]{:S(2)}, u32[]{:S(2)}) collective-permute-start(bf16[2,3,16,512]{3,2,1,0:T(8,128)(2,1)S(1)} %pad_maximum_fusion.3), channel_id=1, source_target_pairs={{1,2},{2,1},{3,4},{4,3},{5,6},{6,5},{7,8},{8,7},{9,10},{10,9},{11,... | collective-permute-start | bytes 294920 | tf_op jit(solution)/shard_map/ppermute | solution.py:279
  5.2 5.0 %collective-permute-start.4 = (bf16[2,3,32,512]{3,2,1,0:T(8,128)(2,1)S(1)}, bf16[2,3,32,512]{3,2,1,0:T(8,128)(2,1)S(1)}, u32[]{:S(2)}, u32[]{:S(2)}) collective-permute-start(bf16[2,3,32,512]{3,2,1,0:T(8,128)(2,1)S(1)} %slice.39), channel_id=1, source_target_pairs={{1,2},{2,1},{3,4},{4,3},{5,6},{6,5},{7,8},{8,7},{9,10},{10,9},{11,... | collective-permute-start | bytes 589832 | tf_op jit(solution)/shard_map/ppermute | solution.py:280
  10.2 0.1 collective-permute-start.1
  10.3 0.2 collective-permute-done
  10.5 1.3 %collective-permute-done.1.ri = bf16[2,3,48,512]{3,2,1,0:T(8,128)(2,1)S(1)} collective-permute-done((bf16[2,3,48,512]{3,2,1,0:T(8,128)(2,1)S(1)}, bf16[2,3,48,512]{3,2,1,0:T(8,128)(2,1)S(1)}, u32[]{:S(2)}, u32[]{:S(2)}) %collective-permute-start.1) | collective-permute-done | bytes 294944 | tf_op jit(solution)/shard_map/ppermute | solution.py:278
  11.9 0.1 pad_maximum_fusion.1
  11.9 1.6 %collective-permute-start.2 = (bf16[192,512]{1,0:T(8,128)(2,1)S(1)}, bf16[192,512]{1,0:T(8,128)(2,1)S(1)}, u32[]{:S(2)}, u32[]{:S(2)}) collective-permute-start(bf16[192,512]{1,0:T(8,128)(2,1)S(1)} %bitcast.13), channel_id=1, source_target_pairs={{0,64},{64,128},{128,192},{192,0},{1,65},{65,129},{129,193},{193,1... | collective-permute-start | bytes 589832 | tf_op jit(solution)/shard_map/ppermute | solution.py:264
  13.5 1.7 %collective-permute-start.3 = (bf16[192,512]{1,0:T(8,128)(2,1)S(1)}, bf16[192,512]{1,0:T(8,128)(2,1)S(1)}, u32[]{:S(2)}, u32[]{:S(2)}) collective-permute-start(bf16[192,512]{1,0:T(8,128)(2,1)S(1)} %bitcast.12), channel_id=1, source_target_pairs={{0,192},{64,0},{128,64},{192,128},{1,193},{65,1},{129,65},{193,129... | collective-permute-start | bytes 589832 | tf_op jit(solution)/shard_map/ppermute | solution.py:264
  15.2 0.0 copy-done.2
  15.2 0.0 copy-done.5
  15.3 0.0 copy-done.8
  15.3 0.0 copy-start.1
  15.3 4.2 %own_cells.1 = (f32[2,3,48,512]{3,2,1,0:T(8,128)S(1)}, f32[2,3,48,512]{3,2,1,0:T(8,128)S(1)}, bf16[2,3,48,512]{3,2,1,0:T(8,128)(2,1)S(1)}, bf16[2,3,48,512]{3,2,...) custom-call(bf16[2,3,48,512]{3,2,1,0:T(8,128)(2,1)S(1)} %get-tuple-element.20.xj, ...), custom_call_target="tpu_custom_call" | custom-call | flops 3000000000 | bytes 4000000 | tf_op jit(solution)/shard_map/own_cells/pallas_call | solution.py:295
  19.5 0.0 copy-start
  19.5 0.0 copy-start.3
  19.5 0.0 copy-start.4
  19.5 0.0 copy-start.6
  19.5 0.0 collective-permute-done.4
  19.6 2.9 %far_rows.1 = (f32[2,3,48,512]{3,2,1,0:T(8,128)S(1)}, f32[2,3,48,512]{3,2,1,0:T(8,128)S(1)}) custom-call(bf16[2,3,48,512]{3,2,1,0:T(8,128)(2,1)S(1)} %pad_maximum_fusion.rj, bf16[512,1536]{1,0:T(8,128)(2,1)S(1)} %copy-done.2, f32[1,512]{1,0:T(1,128)S(1)} %bitcast.8, f32[2,3,48,512]{3,2,1,0:T(8,128)S(1)} %get-tuple-element.26.qj, ...), custom_call_target="tpu_custom_call" | custom-call | flops 2000000000 | bytes 4000000 | tf_op jit(solution)/shard_map/far_rows/pallas_call | solution.py:307
  22.4 0.0 collective-permute-done.2.left
  22.4 0.0 collective-permute-done.3.right
  22.5 0.0 copy-done.1
  22.5 0.0 copy-done
  22.5 0.0 copy-done.3
  22.5 0.0 copy-done.4
  22.5 0.0 copy-done.6
  22.5 5.3 %edges_merge_split.1 = bf16[2,6,48,512]{3,2,1,0:T(8,128)(2,1)} custom-call(bf16[192,512]{1,0:T(8,128)(2,1)S(1)} %collective-permute-done.2.left, bf16[192,512]{1,0:T(8,128)(2,1)S(1)} %collective-permute-done.3.right, bf16[2,3,48,512]{3,2,1,0:T(8,128)(2,1)S(1)} %get-tuple-element.20.xj, bf16[2,3,48,512]{3,2,1,0:T(8,128)(2,1)S(1)} %get-tuple-element.21.xi, ...), custom_call_target="tpu_custom_call" | custom-call | flops 3000000000 | bytes 12000000 | tf_op jit(solution)/shard_map/edges_merge_split/pallas_call | solution.py:317
  (8 shorter events, 0.1 us)
Async XLA Ops:
  0.0 15.2 %copy-start.2 = (bf16[512,1536]{1,0:T(8,128)(2,1)S(1)}, bf16[512,1536]{1,0:T(8,128)(2,1)}, u32[]{:S(2)}) copy-start(bf16[512,1536]{1,0:T(8,128)(2,1)} %qkv.1) | copy-start | bytes 4718596
  0.0 15.2 %copy-start.5 = (f32[512]{0:T(512)S(1)}, f32[512]{0:T(512)}, u32[]{:S(2)}) copy-start(f32[512]{0:T(512)} %param.12) | copy-start | bytes 6148
  0.0 1.2 %copy-start.7 = (bf16[2,6,48,512]{3,2,1,0:T(8,128)(2,1)S(1)}, bf16[2,6,48,512]{3,2,1,0:T(8,128)(2,1)}, u32[]{:S(2)}) copy-start(bf16[2,6,48,512]{3,2,1,0:T(8,128)(2,1)} %tokens.1) | copy-start | bytes 1769476
  1.2 14.1 %copy-start.8 = (f32[8]{0:T(128)S(1)}, f32[8]{0:T(128)}, u32[]{:S(2)}) copy-start(f32[8]{0:T(128)} %param.13) | copy-start | bytes 100
  1.3 9.3 %collective-permute-start = (bf16[2,3,16,512]{3,2,1,0:T(8,128)(2,1)S(1)}, bf16[2,3,16,512]{3,2,1,0:T(8,128)(2,1)S(1)}, u32[]{:S(2)}, u32[]{:S(2)}) collective-permute-start(bf16[2,3,16,512]{3,2,1,0:T(8,128)(2,1)S(1)} %pad_maximum_fusion.3), channel_id=1, source_target_pairs={{1,2},{2,1},{3,4},{4,3},{5,6},{6,5},{7,8},{8,7},{9,10},{10,9},{11,... | collective-permute-start | bytes 294920 | tf_op jit(solution)/shard_map/ppermute | solution.py:279
  5.2 14.3 %collective-permute-start.4 = (bf16[2,3,32,512]{3,2,1,0:T(8,128)(2,1)S(1)}, bf16[2,3,32,512]{3,2,1,0:T(8,128)(2,1)S(1)}, u32[]{:S(2)}, u32[]{:S(2)}) collective-permute-start(bf16[2,3,32,512]{3,2,1,0:T(8,128)(2,1)S(1)} %slice.39), channel_id=1, source_target_pairs={{1,2},{2,1},{3,4},{4,3},{5,6},{6,5},{7,8},{8,7},{9,10},{10,9},{11,... | collective-permute-start | bytes 589832 | tf_op jit(solution)/shard_map/ppermute | solution.py:280
  10.2 1.7 %collective-permute-start.1 = (bf16[2,3,48,512]{3,2,1,0:T(8,128)(2,1)S(1)}, bf16[2,3,48,512]{3,2,1,0:T(8,128)(2,1)S(1)}, u32[]{:S(2)}, u32[]{:S(2)}) collective-permute-start(bf16[2,3,48,512]{3,2,1,0:T(8,128)(2,1)S(1)} %get-tuple-element.21.xi), channel_id=1, source_target_pairs={{0,1},{1,0},{2,3},{3,2},{4,5},{5,4},{6,7},{7,6},{8,9},{9,8},{10,11... | collective-permute-start | bytes 884744 | tf_op jit(solution)/shard_map/ppermute | solution.py:278
  11.9 10.5 %collective-permute-start.2 = (bf16[192,512]{1,0:T(8,128)(2,1)S(1)}, bf16[192,512]{1,0:T(8,128)(2,1)S(1)}, u32[]{:S(2)}, u32[]{:S(2)}) collective-permute-start(bf16[192,512]{1,0:T(8,128)(2,1)S(1)} %bitcast.13), channel_id=1, source_target_pairs={{0,64},{64,128},{128,192},{192,0},{1,65},{65,129},{129,193},{193,1... | collective-permute-start | bytes 589832 | tf_op jit(solution)/shard_map/ppermute | solution.py:264
  13.5 8.9 %collective-permute-start.3 = (bf16[192,512]{1,0:T(8,128)(2,1)S(1)}, bf16[192,512]{1,0:T(8,128)(2,1)S(1)}, u32[]{:S(2)}, u32[]{:S(2)}) collective-permute-start(bf16[192,512]{1,0:T(8,128)(2,1)S(1)} %bitcast.12), channel_id=1, source_target_pairs={{0,192},{64,0},{128,64},{192,128},{1,193},{65,1},{129,65},{193,129... | collective-permute-start | bytes 589832 | tf_op jit(solution)/shard_map/ppermute | solution.py:264
  15.3 7.2 %copy-start.1 = (bf16[1024,2048]{1,0:T(8,128)(2,1)S(1)}, bf16[1024,2048]{1,0:T(8,128)(2,1)}, u32[]{:S(2)}) copy-start(bf16[1024,2048]{1,0:T(8,128)(2,1)} %split_weight.1) | copy-start | bytes 12582916
  19.5 3.0 %copy-start = (bf16[2048,1024]{1,0:T(8,128)(2,1)S(1)}, bf16[2048,1024]{1,0:T(8,128)(2,1)}, u32[]{:S(2)}) copy-start(bf16[2048,1024]{1,0:T(8,128)(2,1)} %merge_weight.1) | copy-start | bytes 12582916
  19.5 3.0 %copy-start.3 = (bf16[512,512]{1,0:T(8,128)(2,1)S(1)}, bf16[512,512]{1,0:T(8,128)(2,1)}, u32[]{:S(2)}) copy-start(bf16[512,512]{1,0:T(8,128)(2,1)} %out_weight.1) | copy-start | bytes 1572868
  19.5 3.0 %copy-start.4 = (f32[2048]{0:T(1024)S(1)}, f32[2048]{0:T(1024)}, u32[]{:S(2)}) copy-start(f32[2048]{0:T(1024)} %param.15) | copy-start | bytes 24580
  19.5 3.0 %copy-start.6 = (f32[512]{0:T(512)S(1)}, f32[512]{0:T(512)}, u32[]{:S(2)}) copy-start(f32[512]{0:T(512)} %param.17) | copy-start | bytes 6148

commit v2 on v1

v2 whole, which is shorter than its diff:
```python
import jax
import jax.numpy as jnp
from jax import lax
from jax.experimental import pallas as pl
from jax.experimental.pallas import tpu as pltpu
from jax.sharding import PartitionSpec as P

BF = jnp.bfloat16
F32 = jnp.float32
D = 512
LOG2E = 1.4426950408889634
VMEM = pl.BlockSpec(memory_space=pltpu.VMEM)
PARAMS = pltpu.CompilerParams(vmem_limit_bytes=24 * 2**20)


def dot(a, b):
    return jnp.dot(a, b, preferred_element_type=F32)


def dot_t(a, b):
    return lax.dot_general(a, b, (((1,), (1,)), ((), ())), preferred_element_type=F32)


def layer_norm(value, gain):
    centered = value - jnp.mean(value, -1, keepdims=True)
    variance = jnp.mean(centered * centered, -1, keepdims=True)
    return centered * lax.rsqrt(variance + 1e-05) * gain


def head_scaled(value, block, extra=None):
    rounded = value.astype(BF)
    squares = rounded * rounded
    sums = jnp.concatenate([dot(squares[:, :256], block), dot(squares[:, 256:], block)], 1)
    inverse = lax.rsqrt(sums + 1e-06)
    return value * (inverse if extra is None else inverse * extra)


def stack_heads(q):
    lane = lax.broadcasted_iota(jnp.int32, q.shape, 1)
    return jnp.concatenate(
        [jnp.where((lane >= 64 * h) & (lane < 64 * h + 64), q, 0.0) for h in range(4)], 0
    ).astype(BF)


def unstack_heads(value, m):
    lane = lax.broadcasted_iota(jnp.int32, (m, 128), 1)
    halves = []
    for g in range(2):
        col = slice(128 * g, 128 * g + 128) if value.shape[1] > 1 else slice(None)
        first = value[2 * g * m : (2 * g + 1) * m, col]
        second = value[(2 * g + 1) * m : (2 * g + 2) * m, col]
        halves.append(jnp.where(lane < 64, first, second))
    return jnp.concatenate(halves, 1)


def scores_to_sums(q, k, v, mask):
    m = q.shape[0]
    weight = jnp.exp2(dot_t(stack_heads(q), k)) * mask
    total = jnp.sum(weight, 1, keepdims=True)
    return unstack_heads(dot(weight.astype(BF), v), m), unstack_heads(total, m)


def window(col):
    return lax.shift_right_logical((col + 18) * 5462, 16)


def present_rows():
    lat = lax.axis_index("lat")
    return jnp.where((lat > 0) & (lat < lax.axis_size("lat") - 1), 1.0, 0.0)


def main_mask(ch, present):
    query = lax.broadcasted_iota(jnp.int32, (72, 192), 0)
    key = lax.broadcasted_iota(jnp.int32, (72, 192), 1)
    row = (query >= 24).astype(jnp.int32) + (query >= 48).astype(jnp.int32)
    same = window(24 * ch + query - 24 * row) == window(16 * ch + (key & 31))
    value = jnp.where(same, jnp.where(key < 96, 1.0, present), 0.0)
    return jnp.concatenate([value] * 4, 0)


def edge_mask(side):
    query = lax.broadcasted_iota(jnp.int32, (96, 144), 0)
    key = lax.broadcasted_iota(jnp.int32, (96, 144), 1)
    same = window(40 * side + (query & 7)) == window((48 if side else -8) + (key & 7))
    keep = query < 0
    for group, (low, high) in enumerate(((0, 24), (72, 96), (24, 72), (96, 144))):
        rows = (query >= 24 * group) & (query < 24 * group + 24)
        keep = keep | (rows & (key >= low) & (key < high))
    return jnp.concatenate([jnp.where(same & keep, 1.0, 0.0)] * 4, 0)


def corner_mask(present):
    query = lax.broadcasted_iota(jnp.int32, (96, 96), 0)
    key = lax.broadcasted_iota(jnp.int32, (96, 96), 1)
    keep = query < 0
    for group in range(4):
        side = group // 2
        rows = (query >= 24 * group) & (query < 24 * group + 24)
        keys = (key >= 24 * group) & (key < 24 * group + 24)
        same = window(40 * side + (query & 7)) == window((48 if side else -8) + (key & 7))
        keep = keep | (rows & keys & same)
    return jnp.concatenate([jnp.where(keep, present, 0.0)] * 4, 0)


def head_blocks():
    row = lax.broadcasted_iota(jnp.int32, (256, 256), 0)
    lane = lax.broadcasted_iota(jnp.int32, (256, 256), 1)
    same = lax.shift_right_logical(row, 6) == lax.shift_right_logical(lane, 6)
    return jnp.where(same, 1.0, 0.0).astype(BF)


def attend_half(q, kown, vown, kpart, vpart, present, osum, wsum):
    for ch in range(2):
        mask = main_mask(ch, present)
        for lv in range(2):
            qs = jnp.concatenate([q[lv, r, 24 * ch : 24 * ch + 24] for r in range(3)], 0)
            cells = slice(16 * ch, 16 * ch + 32)
            for hg in range(2):
                feats = slice(256 * hg, 256 * hg + 256)
                k = jnp.concatenate([x[lv, r, cells, feats] for x in (kown, kpart) for r in range(3)], 0)
                v = jnp.concatenate([x[lv, r, cells, feats] for x in (vown, vpart) for r in range(3)], 0)
                o, w = scores_to_sums(qs[:, feats], k, v, mask)
                for r in range(3):
                    osum[lv, r, 24 * ch : 24 * ch + 24, feats] = o[24 * r : 24 * r + 24]
                    wsum[lv, r, 24 * ch : 24 * ch + 24, feats] = w[24 * r : 24 * r + 24]


def project(x_ref, lv, gain, weight, columns):
    normed = layer_norm(x_ref[lv].reshape(144, D).astype(F32), gain).astype(BF)
    return dot(normed, weight[:, columns])


def rows_kernel(tokens, near, far):
    start = 3 * lax.rem(lax.axis_index("lat"), 2)
    near[...] = tokens[:, pl.ds(3 - start, 3)]
    far[...] = tokens[:, pl.ds(start, 3)]


def own_kernel(
    xj, xi, ri, weight, gain, scales, qj, qi, kj, vj, osum, wsum, ki, vi, kr, vr
):
    block = head_blocks()
    lane = lax.broadcasted_iota(jnp.int32, (1, D), 1)
    scale = jnp.zeros((1, D), F32)
    for h in range(8):
        scale = jnp.where(lax.shift_right_logical(lane, 6) == h, scales[:, h : h + 1], scale)
    scale = scale * LOG2E
    for lv in range(2):
        for x, q, k, v in ((xi, qi, ki, vi), (xj, qj, kj, vj)):
            all3 = project(x, lv, gain[...], weight, slice(0, 1536))
            q[lv] = head_scaled(all3[:, :D], block, scale).reshape(3, 48, D)
            k[lv] = head_scaled(all3[:, D : 2 * D], block).astype(BF).reshape(3, 48, D)
            v[lv] = all3[:, 2 * D :].astype(BF).reshape(3, 48, D)
        both = project(ri, lv, gain[...], weight, slice(512, 1536))
        kr[lv] = head_scaled(both[:, :D], block).astype(BF).reshape(3, 48, D)
        vr[lv] = both[:, D:].astype(BF).reshape(3, 48, D)
    attend_half(qi, ki, vi, kr, vr, 1.0, osum, wsum)


def keys_values(tokens, qkv, gain, block):
    normed = layer_norm(tokens.astype(F32), gain).astype(BF)
    both = dot(normed, qkv[:, D:])
    return head_scaled(both[:, :D], block).astype(BF), both[:, D:].astype(BF)


def far_kernel(
    rj, left, right, xj, xi, qkv, gain, out_weight, qj, qi, kj, vj, oi, wi,
    skip, edge_sum, edge_weight, osum, wsum, kr, vr, attended,
):
    block = head_blocks()
    for lv in range(2):
        k, v = keys_values(rj[lv].reshape(144, D), qkv, gain[...], block)
        kr[lv] = k.reshape(3, 48, D)
        vr[lv] = v.reshape(3, 48, D)
    attend_half(qj, kj, vj, kr, vr, present_rows(), osum, wsum)
    mid = slice(8, 40)
    attended[:, :, mid] = oi[:, :, mid] * pl.reciprocal(wi[:, :, mid], approx=True)
    for side, x in enumerate((left, right)):
        k, v = keys_values(x[...], qkv, gain[...], block)
        near = slice(40 * side, 40 * side + 8)
        q = jnp.concatenate(
            [q[lv, r, near] for q in (qj, qi) for lv in range(2) for r in range(3)], 0
        )
        mask = edge_mask(side)
        for hg in range(2):
            feats = slice(256 * hg, 256 * hg + 256)
            oe, we = scores_to_sums(q[:, feats], k[:, feats], v[:, feats], mask)
            for lv in range(2):
                for r in range(3):
                    at = 24 * lv + 8 * r
                    to = slice(48 * side + at, 48 * side + at + 8)
                    edge_sum[to, feats] = osum[lv, r, near, feats] + oe[at : at + 8]
                    edge_weight[to, feats] = wsum[lv, r, near, feats] + we[at : at + 8]
                    total = oi[lv, r, near, feats] + oe[48 + at : 56 + at]
                    weight = wi[lv, r, near, feats] + we[48 + at : 56 + at]
                    attended[lv, r, near, feats] = total * pl.reciprocal(weight, approx=True)
    start = 3 * lax.rem(lax.axis_index("lat"), 2)
    whole = attended[...].reshape(288, D).astype(BF)
    value = xi[...].reshape(288, D).astype(F32) + dot(whole, out_weight[...])
    value = value.astype(BF).astype(F32).reshape(2, 3, 48, D)
    for f in range(4):
        skip[:, pl.ds(3 - start, 3), f] = value[..., 128 * f : 128 * f + 128]
    middle = osum[:, :, mid] * pl.reciprocal(wsum[:, :, mid], approx=True)
    value = dot(middle.reshape(192, D).astype(BF), out_weight[...]).reshape(2, 3, 32, D)
    value = (xj[...].astype(F32)[:, :, mid] + value).astype(BF).astype(F32)
    for f in range(4):
        skip[:, pl.ds(start, 3), f, mid] = value[..., 128 * f : 128 * f + 128]


def last_kernel(
    corners_left, corners_right, xj, qj, edge_sum, edge_weight, most, qkv, gain, out_weight,
    merge_weight, merge_gain, split_weight, split_gain, out, skip, fine, done_rows, sems,
):
    block = head_blocks()
    start = 3 * lax.rem(lax.axis_index("lat"), 2)
    corners = jnp.concatenate([corners_left[...], corners_right[...]], 0)
    k, v = keys_values(corners, qkv, gain[...], block)
    nears = [slice(40 * side, 40 * side + 8) for side in range(2)]
    spots = [(near, lv, r) for near in nears for lv in range(2) for r in range(3)]
    q = jnp.concatenate([qj[lv, r, near] for near, lv, r in spots], 0)
    mask = corner_mask(present_rows())
    attended = []
    for hg in range(2):
        feats = slice(256 * hg, 256 * hg + 256)
        oc, wc = scores_to_sums(q[:, feats], k[:, feats], v[:, feats], mask)
        weight = edge_weight[:, feats] + wc
        attended.append((edge_sum[:, feats] + oc) * pl.reciprocal(weight, approx=True))
    value = dot(jnp.concatenate(attended, 1).astype(BF), out_weight[...])
    own = xj[...].astype(F32)
    skip[...] = most[...]
    for i, (near, lv, r) in enumerate(spots):
        cell = (own[lv, r, near] + value[8 * i : 8 * i + 8]).astype(BF).astype(F32)
        for f in range(4):
            skip[lv, start + r, f, near] = cell[:, 128 * f : 128 * f + 128]
    groups = []
    for c in range(2):
        for r in range(2):
            pieces = []
            for lv in range(2):
                for a in range(3):
                    chunks = [skip[lv, 2 * a + r, f, pl.ds(c, 24, stride=2), :] for f in range(4)]
                    pieces.append(jnp.concatenate(chunks, 1))
            groups.append(jnp.concatenate(pieces, 0))
    mean = sum(jnp.sum(g, -1, keepdims=True) for g in groups) * (1.0 / 2048)
    centered = [g - mean for g in groups]
    variance = sum(jnp.sum(g * g, -1, keepdims=True) for g in centered) * (1.0 / 2048)
    inverse = lax.rsqrt(variance + 1e-05)
    merged = jnp.concatenate(
        [
            (g * inverse * merge_gain[:, D * i : D * i + D]).astype(BF)
            for i, g in enumerate(centered)
        ],
        1,
    )
    coarse = dot(merged, merge_weight[...]).astype(BF)
    copies = []
    for r in range(2):
        for c in range(2):
            i = 2 * c + r
            expanded = dot(coarse, split_weight[:, D * i : D * i + D])
            done = groups[i] + layer_norm(expanded, split_gain[...])
            for lv in range(2):
                for a in range(3):
                    at = (lv * 3 + a) * 24
                    for f in range(4):
                        fine[lv, 2 * a + r, f, pl.ds(c, 24, stride=2), :] = done[
                            at : at + 24, 128 * f : 128 * f + 128
                        ]
        for a in range(3):
            row = 2 * a + r
            for f in range(4):
                done_rows[:, row, :, 128 * f : 128 * f + 128] = fine[:, row, f].astype(BF)
            copies.append(pltpu.make_async_copy(done_rows.at[:, row], out.at[:, row], sems.at[row]))
            copies[-1].start()
    for copy in copies:
        copy.wait()


def body(
    tokens,
    qkv_weight,
    out_weight,
    attn_gain,
    logit_scale,
    merge_weight,
    merge_gain,
    split_weight,
    split_gain,
):
    lats = lax.axis_size("lat")
    pair = [(i, i ^ 1) for i in range(lats)]
    cross = [(i, ((i + 1) ^ 1) - 1) for i in range(1, lats - 1)]

    def along(value, steps):
        count = lax.axis_size("lon")
        return lax.ppermute(value, "lon", [(i, (i + steps) % count) for i in range(count)])

    def cells(dtype):
        return jax.ShapeDtypeStruct((2, 3, 48, D), dtype)

    xi, xj = pl.pallas_call(
        rows_kernel,
        name="rows",
        out_shape=[cells(BF), cells(BF)],
        in_specs=[VMEM],
        out_specs=[VMEM] * 2,
        compiler_params=PARAMS,
        cost_estimate=pl.CostEstimate(flops=5 * 10**9, bytes_accessed=10**6, transcendentals=0),
    )(tokens)
    ri = lax.ppermute(xi, "lat", pair)
    rj = lax.ppermute(xj, "lat", cross)

    def edge_cells(own):
        return jnp.concatenate([xj[:, :, own], xi[:, :, own], ri[:, :, own]], 1).reshape(144, D)

    first, final = slice(0, 8), slice(40, 48)
    to_left, to_right, ri = lax.optimization_barrier((edge_cells(first), edge_cells(final), ri))
    left = along(to_right, 1)
    right = along(to_left, -1)
    gain = attn_gain.reshape(1, D)

    scratch = [pltpu.VMEM((2, 3, 48, D), BF)]
    qj, qi, kj, vj, oi, wi = pl.pallas_call(
        own_kernel,
        name="own_cells",
        out_shape=[cells(F32), cells(F32), cells(BF), cells(BF), cells(F32), cells(F32)],
        in_specs=[VMEM] * 6,
        out_specs=[VMEM] * 6,
        scratch_shapes=scratch * 4,
        compiler_params=PARAMS,
        cost_estimate=pl.CostEstimate(flops=3 * 10**9, bytes_accessed=4 * 10**6, transcendentals=10**6),
    )(xj, xi, ri, qkv_weight, gain, logit_scale.reshape(1, 8))
    corner_left, corner_right, rj, qj = lax.optimization_barrier(
        (rj[:, :, first].reshape(48, D), rj[:, :, final].reshape(48, D), rj, qj)
    )
    corners_left = along(corner_right, 1)
    corners_right = along(corner_left, -1)
    flat = jax.ShapeDtypeStruct((96, D), F32)
    chunked = jax.ShapeDtypeStruct((2, 6, 4, 48, 128), F32)
    most, edge_sum, edge_weight = pl.pallas_call(
        far_kernel,
        name="far_rows_and_edges",
        out_shape=[chunked, flat, flat],
        in_specs=[VMEM] * 14,
        out_specs=[VMEM] * 3,
        scratch_shapes=[pltpu.VMEM((2, 3, 48, D), F32)] * 2
        + [pltpu.VMEM((2, 3, 48, D), BF)] * 2
        + [pltpu.VMEM((2, 3, 48, D), F32)],
        compiler_params=PARAMS,
        cost_estimate=pl.CostEstimate(flops=3 * 10**9, bytes_accessed=4 * 10**6, transcendentals=10**6),
    )(rj, left, right, xj, xi, qkv_weight, gain, out_weight, qj, qi, kj, vj, oi, wi)
    return pl.pallas_call(
        last_kernel,
        name="corners_merge_split",
        out_shape=jax.ShapeDtypeStruct((2, 6, 48, D), BF),
        in_specs=[VMEM] * 14,
        out_specs=pl.BlockSpec(memory_space=pl.ANY),
        scratch_shapes=[
            pltpu.VMEM((2, 6, 4, 48, 128), F32),
            pltpu.VMEM((2, 6, 4, 48, 128), F32),
            pltpu.VMEM((2, 6, 48, D), BF),
            pltpu.SemaphoreType.DMA((6,)),
        ],
        compiler_params=PARAMS,
        cost_estimate=pl.CostEstimate(flops=3 * 10**9, bytes_accessed=12 * 10**6, transcendentals=10**6),
    )(
        corners_left, corners_right, xj, qj, edge_sum, edge_weight, most, qkv_weight, gain, out_weight,
        merge_weight, merge_gain.reshape(1, 4 * D), split_weight, split_gain.reshape(1, D),
    )


def solution(mesh):
    placed = (P(None, "lat", "lon", None), P(), P(), P(), P(), P(), P(), P(), P())
    return jax.shard_map(
        body, mesh=mesh, in_specs=placed, out_specs=P(None, "lat", "lon", None), check_vma=False
    )
```

time: 27.9 us -> 24.3 us (0.87)
  the two profiles are of different devices: /device:TPU:128 before, /device:TPU:192 now
where the time goes in v2:
time: 24.3 us; the launch traced here: 24.2 us
  starting transfers between devices  12.2 us (50%)
  Pallas kernels  10.2 us (42%)
  local copies, waits for them, and re-layouts  1.45 us (6%)
  between operations  0.33 us (1%)
    ppermute x4, starting transfers between devices, along(): lax.ppermute(value, 'lon', [(i, (i + steps) % count) for i in range(count)])  6.63 us
    ppermute x1, starting transfers between devices, body(): rj = lax.ppermute(xj, 'lat', cross)  5.46 us
    pallas_call x1, Pallas kernels, body(): pl.pallas_call(last_kernel, name='corners_merge_split', out_shape=jax.Sha...  3.81 us
    pallas_call x1, Pallas kernels, body(): pl.pallas_call(far_kernel, name='far_rows_and_edges', out_shape=[chunked,...  3.19 us
    pallas_call x1, Pallas kernels, body(): pl.pallas_call(own_kernel, name='own_cells', out_shape=[cells(F32), cells...  3.12 us
    unnamed x18, local copies, waits for them, and re-layouts  1.42 us
  transfers between devices with their start and end apart: 6, of which 0 were waited for; matrix products, arithmetic and copies ran while one was open for 0% of the time, Pallas kernels for 26%

profile of v2, /device:TPU:192, one launch (start us, length us, event | category | flops | bytes accessed | tf_op | source)
XLA Modules:
  0.0 24.2 jit_solution(11901986483713630292)
XLA Ops:
  0.0 0.0 copy-start.2
  0.0 0.0 copy-start.5
  0.0 0.0 copy-start.7
  0.0 1.2 %copy-done.7 = bf16[2,6,48,512]{3,2,1,0:T(8,128)(2,1)S(1)} copy-done((bf16[2,6,48,512]{3,2,1,0:T(8,128)(2,1)S(1)}, bf16[2,6,48,512]{3,2,1,0:T(8,128)(2,1)}, u32[]{:S(2)}) %copy-start.7) | copy-done | bytes 589848
  1.2 0.0 copy-start.8
  1.2 0.1 collective-permute-start.1
  1.3 5.5 %collective-permute-start = (bf16[2,3,48,512]{3,2,1,0:T(8,128)(2,1)S(1)}, bf16[2,3,48,512]{3,2,1,0:T(8,128)(2,1)S(1)}, u32[]{:S(2)}, u32[]{:S(2)}) collective-permute-start(bf16[2,3,48,512]{3,2,1,0:T(8,128)(2,1)S(1)} %get-tuple-element.23.xj), channel_id=1, source_target_pairs={{1,2},{2,1},{3,4},{4,3},{5,6},{6,5},{7,8},{8,7},{9,10},{10,9},{11,... | collective-permute-start | bytes 884744 | tf_op jit(solution)/shard_map/ppermute | solution.py:311
  6.8 0.0 collective-permute-done.1.ri
  6.9 1.6 %collective-permute-start.4 = (bf16[144,512]{1,0:T(8,128)(2,1)S(1)}, bf16[144,512]{1,0:T(8,128)(2,1)S(1)}, u32[]{:S(2)}, u32[]{:S(2)}) collective-permute-start(bf16[144,512]{1,0:T(8,128)(2,1)S(1)} %bitcast.15), channel_id=1, source_target_pairs={{0,64},{64,128},{128,192},{192,0},{1,65},{65,129},{129,193},{193,1... | collective-permute-start | bytes 442376 | tf_op jit(solution)/shard_map/ppermute | solution.py:296
  8.5 1.7 %collective-permute-start.5 = (bf16[144,512]{1,0:T(8,128)(2,1)S(1)}, bf16[144,512]{1,0:T(8,128)(2,1)S(1)}, u32[]{:S(2)}, u32[]{:S(2)}) collective-permute-start(bf16[144,512]{1,0:T(8,128)(2,1)S(1)} %bitcast.14), channel_id=1, source_target_pairs={{0,192},{64,0},{128,64},{192,128},{1,193},{65,1},{129,65},{193,129... | collective-permute-start | bytes 442376 | tf_op jit(solution)/shard_map/ppermute | solution.py:296
  10.2 0.0 copy-done.2
  10.2 0.0 copy-done.5
  10.2 0.0 copy-done.8
  10.2 0.0 copy-start.3
  10.2 3.1 %own_cells.1 = (f32[2,3,48,512]{3,2,1,0:T(8,128)S(1)}, f32[2,3,48,512]{3,2,1,0:T(8,128)S(1)}, bf16[2,3,48,512]{3,2,1,0:T(8,128)(2,1)S(1)}, bf16[2,3,48,512]{3,2,...) custom-call(bf16[2,3,48,512]{3,2,1,0:T(8,128)(2,1)S(1)} %get-tuple-element.23.xj, ...), custom_call_target="tpu_custom_call" | custom-call | flops 3000000000 | bytes 4000000 | tf_op jit(solution)/shard_map/own_cells/pallas_call | solution.py:323
  13.4 0.0 collective-permute-done.rj
  13.4 0.4 %collective-permute-start.2 = (bf16[48,512]{1,0:T(8,128)(2,1)S(1)}, bf16[48,512]{1,0:T(8,128)(2,1)S(1)}, u32[]{:S(2)}, u32[]{:S(2)}) collective-permute-start(bf16[48,512]{1,0:T(8,128)(2,1)S(1)} %bitcast.17), channel_id=1, source_target_pairs={{0,64},{64,128},{128,192},{192,0},{1,65},{65,129},{129,193},{193,1... | collective-permute-start | bytes 147464 | tf_op jit(solution)/shard_map/ppermute | solution.py:296
  13.7 3.0 %collective-permute-start.3 = (bf16[48,512]{1,0:T(8,128)(2,1)S(1)}, bf16[48,512]{1,0:T(8,128)(2,1)S(1)}, u32[]{:S(2)}, u32[]{:S(2)}) collective-permute-start(bf16[48,512]{1,0:T(8,128)(2,1)S(1)} %bitcast.16), channel_id=1, source_target_pairs={{0,192},{64,0},{128,64},{192,128},{1,193},{65,1},{129,65},{193,129... | collective-permute-start | bytes 147464 | tf_op jit(solution)/shard_map/ppermute | solution.py:296
  16.7 0.0 collective-permute-done.4.left
  16.7 0.0 collective-permute-done.5.right
  16.7 0.0 copy-done.3
  16.7 0.0 copy-start
  16.7 0.0 copy-start.1
  16.7 0.0 copy-start.4
  16.7 0.0 copy-start.6
  16.8 3.2 %far_rows_and_edges.1 = (f32[2,6,4,48,128]{4,3,2,1,0:T(8,128)S(1)}, f32[96,512]{1,0:T(8,128)S(1)}, f32[96,512]{1,0:T(8,128)S(1)}) custom-call(bf16[2,3,48,512]{3,2,1,0:T(8,128)(2,1)S(1)} %collective-permute-done.rj, bf16[144,512]{1,0:T(8,128)(2,1)S(1)} %collective-permute-done.4.left, bf16[144,512]{1,0:T(8,128)(2,1)S(1)} %collective-permute-done.5.right, ...), custom_call_target="tpu_custom_call" | custom-call | flops 3000000000 | bytes 4000000 | tf_op jit(solution)/shard_map/far_rows_and_edges/pallas_call | solution.py:340
  20.0 0.0 collective-permute-done.2.corners_left
  20.0 0.0 collective-permute-done.3.corners_right
  20.0 0.0 copy-done
  20.0 0.2 copy-done.1
  20.2 0.0 copy-done.4
  20.2 0.0 copy-done.6
  20.2 3.8 %corners_merge_split.1 = bf16[2,6,48,512]{3,2,1,0:T(8,128)(2,1)} custom-call(bf16[48,512]{1,0:T(8,128)(2,1)S(1)} %collective-permute-done.2.corners_left, bf16[48,512]{1,0:T(8,128)(2,1)S(1)} %collective-permute-done.3.corners_right, bf16[2,3,48,512]{3,2,1,0:T(8,128)(2,1)S(1)} %get-tuple-element.23.xj, f32[2,3,48,512]{3,2,1,0:T(8,128)S(1)} %get-tuple-element.29.qj, ...), custom_call_target="tpu_custom_call" | custom-call | flops 3000000000 | bytes 12000000 | tf_op jit(solution)/shard_map/corners_merge_split/pallas_call | solution.py:352
  (6 shorter events, 0.1 us)
Async XLA Ops:
  0.0 10.2 %copy-start.2 = (bf16[512,1536]{1,0:T(8,128)(2,1)S(1)}, bf16[512,1536]{1,0:T(8,128)(2,1)}, u32[]{:S(2)}) copy-start(bf16[512,1536]{1,0:T(8,128)(2,1)} %qkv.3) | copy-start | bytes 4718596
  0.0 10.2 %copy-start.5 = (f32[512]{0:T(512)S(1)}, f32[512]{0:T(512)}, u32[]{:S(2)}) copy-start(f32[512]{0:T(512)} %param.12) | copy-start | bytes 6148
  0.0 1.2 %copy-start.7 = (bf16[2,6,48,512]{3,2,1,0:T(8,128)(2,1)S(1)}, bf16[2,6,48,512]{3,2,1,0:T(8,128)(2,1)}, u32[]{:S(2)}) copy-start(bf16[2,6,48,512]{3,2,1,0:T(8,128)(2,1)} %tokens.1) | copy-start | bytes 1769476
  1.2 9.0 %copy-start.8 = (f32[8]{0:T(128)S(1)}, f32[8]{0:T(128)}, u32[]{:S(2)}) copy-start(f32[8]{0:T(128)} %param.13) | copy-start | bytes 100
  1.2 5.6 %collective-permute-start.1 = (bf16[2,3,48,512]{3,2,1,0:T(8,128)(2,1)S(1)}, bf16[2,3,48,512]{3,2,1,0:T(8,128)(2,1)S(1)}, u32[]{:S(2)}, u32[]{:S(2)}) collective-permute-start(bf16[2,3,48,512]{3,2,1,0:T(8,128)(2,1)S(1)} %get-tuple-element.24.xi), channel_id=1, source_target_pairs={{0,1},{1,0},{2,3},{3,2},{4,5},{5,4},{6,7},{7,6},{8,9},{9,8},{10,11... | collective-permute-start | bytes 884744 | tf_op jit(solution)/shard_map/ppermute | solution.py:310
  1.3 12.0 %collective-permute-start = (bf16[2,3,48,512]{3,2,1,0:T(8,128)(2,1)S(1)}, bf16[2,3,48,512]{3,2,1,0:T(8,128)(2,1)S(1)}, u32[]{:S(2)}, u32[]{:S(2)}) collective-permute-start(bf16[2,3,48,512]{3,2,1,0:T(8,128)(2,1)S(1)} %get-tuple-element.23.xj), channel_id=1, source_target_pairs={{1,2},{2,1},{3,4},{4,3},{5,6},{6,5},{7,8},{8,7},{9,10},{10,9},{11,... | collective-permute-start | bytes 884744 | tf_op jit(solution)/shard_map/ppermute | solution.py:311
  6.9 9.8 %collective-permute-start.4 = (bf16[144,512]{1,0:T(8,128)(2,1)S(1)}, bf16[144,512]{1,0:T(8,128)(2,1)S(1)}, u32[]{:S(2)}, u32[]{:S(2)}) collective-permute-start(bf16[144,512]{1,0:T(8,128)(2,1)S(1)} %bitcast.15), channel_id=1, source_target_pairs={{0,64},{64,128},{128,192},{192,0},{1,65},{65,129},{129,193},{193,1... | collective-permute-start | bytes 442376 | tf_op jit(solution)/shard_map/ppermute | solution.py:296
  8.5 8.2 %collective-permute-start.5 = (bf16[144,512]{1,0:T(8,128)(2,1)S(1)}, bf16[144,512]{1,0:T(8,128)(2,1)S(1)}, u32[]{:S(2)}, u32[]{:S(2)}) collective-permute-start(bf16[144,512]{1,0:T(8,128)(2,1)S(1)} %bitcast.14), channel_id=1, source_target_pairs={{0,192},{64,0},{128,64},{192,128},{1,193},{65,1},{129,65},{193,129... | collective-permute-start | bytes 442376 | tf_op jit(solution)/shard_map/ppermute | solution.py:296
  10.2 6.5 %copy-start.3 = (bf16[512,512]{1,0:T(8,128)(2,1)S(1)}, bf16[512,512]{1,0:T(8,128)(2,1)}, u32[]{:S(2)}) copy-start(bf16[512,512]{1,0:T(8,128)(2,1)} %out_weight.3) | copy-start | bytes 1572868
  13.4 6.6 %collective-permute-start.2 = (bf16[48,512]{1,0:T(8,128)(2,1)S(1)}, bf16[48,512]{1,0:T(8,128)(2,1)S(1)}, u32[]{:S(2)}, u32[]{:S(2)}) collective-permute-start(bf16[48,512]{1,0:T(8,128)(2,1)S(1)} %bitcast.17), channel_id=1, source_target_pairs={{0,64},{64,128},{128,192},{192,0},{1,65},{65,129},{129,193},{193,1... | collective-permute-start | bytes 147464 | tf_op jit(solution)/shard_map/ppermute | solution.py:296
  13.7 6.2 %collective-permute-start.3 = (bf16[48,512]{1,0:T(8,128)(2,1)S(1)}, bf16[48,512]{1,0:T(8,128)(2,1)S(1)}, u32[]{:S(2)}, u32[]{:S(2)}) collective-permute-start(bf16[48,512]{1,0:T(8,128)(2,1)S(1)} %bitcast.16), channel_id=1, source_target_pairs={{0,192},{64,0},{128,64},{192,128},{1,193},{65,1},{129,65},{193,129... | collective-permute-start | bytes 147464 | tf_op jit(solution)/shard_map/ppermute | solution.py:296
  16.7 3.3 %copy-start = (bf16[2048,1024]{1,0:T(8,128)(2,1)S(1)}, bf16[2048,1024]{1,0:T(8,128)(2,1)}, u32[]{:S(2)}) copy-start(bf16[2048,1024]{1,0:T(8,128)(2,1)} %merge_weight.1) | copy-start | bytes 12582916
  16.7 3.5 %copy-start.1 = (bf16[1024,2048]{1,0:T(8,128)(2,1)S(1)}, bf16[1024,2048]{1,0:T(8,128)(2,1)}, u32[]{:S(2)}) copy-start(bf16[1024,2048]{1,0:T(8,128)(2,1)} %split_weight.1) | copy-start | bytes 12582916
  16.7 3.5 %copy-start.4 = (f32[2048]{0:T(1024)S(1)}, f32[2048]{0:T(1024)}, u32[]{:S(2)}) copy-start(f32[2048]{0:T(1024)} %param.15) | copy-start | bytes 24580
  16.7 3.4 %copy-start.6 = (f32[512]{0:T(512)S(1)}, f32[512]{0:T(512)}, u32[]{:S(2)}) copy-start(f32[512]{0:T(512)} %param.17) | copy-start | bytes 6148

commit v3 on v2

--- a/solution.py
+++ b/solution.py
@@ -69,24 +69,20 @@
     return jnp.where((lat > 0) & (lat < lax.axis_size("lat") - 1), 1.0, 0.0)
 
 
-def main_mask(ch, present):
-    query = lax.broadcasted_iota(jnp.int32, (72, 192), 0)
-    key = lax.broadcasted_iota(jnp.int32, (72, 192), 1)
+def window_mask(ch, lv, near, present):
+    query = lax.broadcasted_iota(jnp.int32, (72, 240), 0)
+    key = lax.broadcasted_iota(jnp.int32, (72, 240), 1)
     row = (query >= 24).astype(jnp.int32) + (query >= 48).astype(jnp.int32)
-    same = window(24 * ch + query - 24 * row) == window(16 * ch + (key & 31))
-    value = jnp.where(same, jnp.where(key < 96, 1.0, present), 0.0)
+    edge = key >= 192
+    column = jnp.where(edge, (48 if ch else -8) + (key & 7), 16 * ch + (key & 31))
+    same = window(24 * ch + query - 24 * row) == window(column)
+    if near:
+        value = jnp.where(same, 1.0, 0.0)
+    else:
+        other = (key >= 96) & (key < 192)
+        level = (key < 216) if lv == 0 else (key < 192) | (key >= 216)
+        value = jnp.where(same & level, jnp.where(other, present, 1.0), 0.0)
     return jnp.concatenate([value] * 4, 0)
-
-
-def edge_mask(side):
-    query = lax.broadcasted_iota(jnp.int32, (96, 144), 0)
-    key = lax.broadcasted_iota(jnp.int32, (96, 144), 1)
-    same = window(40 * side + (query & 7)) == window((48 if side else -8) + (key & 7))
-    keep = query < 0
-    for group, (low, high) in enumerate(((0, 24), (72, 96), (24, 72), (96, 144))):
-        rows = (query >= 24 * group) & (query < 24 * group + 24)
-        keep = keep | (rows & (key >= low) & (key < high))
-    return jnp.concatenate([jnp.where(same & keep, 1.0, 0.0)] * 4, 0)
 
 
 def corner_mask(present):
@@ -109,20 +105,23 @@
     return jnp.where(same, 1.0, 0.0).astype(BF)
 
 
-def attend_half(q, kown, vown, kpart, vpart, present, osum, wsum):
+def attend_half(q, kown, vown, kpart, vpart, kedge, vedge, near, present, store):
     for ch in range(2):
-        mask = main_mask(ch, present)
         for lv in range(2):
+            mask = window_mask(ch, lv, near, present)
             qs = jnp.concatenate([q[lv, r, 24 * ch : 24 * ch + 24] for r in range(3)], 0)
             cells = slice(16 * ch, 16 * ch + 32)
+            edge = slice(48 * lv, 48 * lv + 48) if near else slice(96, 144)
             for hg in range(2):
                 feats = slice(256 * hg, 256 * hg + 256)
-                k = jnp.concatenate([x[lv, r, cells, feats] for x in (kown, kpart) for r in range(3)], 0)
-                v = jnp.concatenate([x[lv, r, cells, feats] for x in (vown, vpart) for r in range(3)], 0)
+                k = [x[lv, r, cells, feats] for x in (kown, kpart) for r in range(3)]
+                v = [x[lv, r, cells, feats] for x in (vown, vpart) for r in range(3)]
+                k = jnp.concatenate(k + [kedge[ch, edge, feats]], 0)
+                v = jnp.concatenate(v + [vedge[ch, edge, feats]], 0)
                 o, w = scores_to_sums(qs[:, feats], k, v, mask)
                 for r in range(3):
-                    osum[lv, r, 24 * ch : 24 * ch + 24, feats] = o[24 * r : 24 * r + 24]
-                    wsum[lv, r, 24 * ch : 24 * ch + 24, feats] = w[24 * r : 24 * r + 24]
+                    rows = slice(24 * r, 24 * r + 24)
+                    store(lv, r, slice(24 * ch, 24 * ch + 24), feats, o[rows], w[rows])
 
 
 def project(x_ref, lv, gain, weight, columns):
@@ -136,9 +135,7 @@
     far[...] = tokens[:, pl.ds(start, 3)]
 
 
-def own_kernel(
-    xj, xi, ri, weight, gain, scales, qj, qi, kj, vj, osum, wsum, ki, vi, kr, vr
-):
+def own_kernel(xj, xi, ri, weight, gain, scales, qj, qi, kj, vj, ki, vi, kr, vr):
     block = head_blocks()
     lane = lax.broadcasted_iota(jnp.int32, (1, D), 1)
     scale = jnp.zeros((1, D), F32)
@@ -154,7 +151,6 @@
         both = project(ri, lv, gain[...], weight, slice(512, 1536))
         kr[lv] = head_scaled(both[:, :D], block).astype(BF).reshape(3, 48, D)
         vr[lv] = both[:, D:].astype(BF).reshape(3, 48, D)
-    attend_half(qi, ki, vi, kr, vr, 1.0, osum, wsum)
 
 
 def keys_values(tokens, qkv, gain, block):
@@ -164,36 +160,34 @@
 
 
 def far_kernel(
-    rj, left, right, xj, xi, qkv, gain, out_weight, qj, qi, kj, vj, oi, wi,
-    skip, edge_sum, edge_weight, osum, wsum, kr, vr, attended,
+    rj, left, right, xj, xi, qkv, gain, out_weight, qj, qi, kj, vj, ki, vi, kn, vn,
+    skip, edge_sum, edge_weight, osum, wsum, kr, vr, ke, ve, attended,
 ):
     block = head_blocks()
+    mid = slice(8, 40)
+    for side, x in enumerate((left, right)):
+        ke[side], ve[side] = keys_values(x[...], qkv, gain[...], block)
     for lv in range(2):
         k, v = keys_values(rj[lv].reshape(144, D), qkv, gain[...], block)
         kr[lv] = k.reshape(3, 48, D)
         vr[lv] = v.reshape(3, 48, D)
-    attend_half(qj, kj, vj, kr, vr, present_rows(), osum, wsum)
-    mid = slice(8, 40)
-    attended[:, :, mid] = oi[:, :, mid] * pl.reciprocal(wi[:, :, mid], approx=True)
-    for side, x in enumerate((left, right)):
-        k, v = keys_values(x[...], qkv, gain[...], block)
+
+    def finish(lv, r, columns, feats, o, w):
+        attended[lv, r, columns, feats] = o * pl.reciprocal(w, approx=True)
+
+    def keep(lv, r, columns, feats, o, w):
+        osum[lv, r, columns, feats] = o
+        wsum[lv, r, columns, feats] = w
+
+    attend_half(qi, ki, vi, kn, vn, ke, ve, True, 1.0, finish)
+    attend_half(qj, kj, vj, kr, vr, ke, ve, False, present_rows(), keep)
+    for side in range(2):
         near = slice(40 * side, 40 * side + 8)
-        q = jnp.concatenate(
-            [q[lv, r, near] for q in (qj, qi) for lv in range(2) for r in range(3)], 0
-        )
-        mask = edge_mask(side)
-        for hg in range(2):
-            feats = slice(256 * hg, 256 * hg + 256)
-            oe, we = scores_to_sums(q[:, feats], k[:, feats], v[:, feats], mask)
-            for lv in range(2):
-                for r in range(3):
-                    at = 24 * lv + 8 * r
-                    to = slice(48 * side + at, 48 * side + at + 8)
-                    edge_sum[to, feats] = osum[lv, r, near, feats] + oe[at : at + 8]
-                    edge_weight[to, feats] = wsum[lv, r, near, feats] + we[at : at + 8]
-                    total = oi[lv, r, near, feats] + oe[48 + at : 56 + at]
-                    weight = wi[lv, r, near, feats] + we[48 + at : 56 + at]
-                    attended[lv, r, near, feats] = total * pl.reciprocal(weight, approx=True)
+        for lv in range(2):
+            for r in range(3):
+                to = slice(48 * side + 24 * lv + 8 * r, 48 * side + 24 * lv + 8 * r + 8)
+                edge_sum[to] = osum[lv, r, near]
+                edge_weight[to] = wsum[lv, r, near]
     start = 3 * lax.rem(lax.axis_index("lat"), 2)
     whole = attended[...].reshape(288, D).astype(BF)
     value = xi[...].reshape(288, D).astype(F32) + dot(whole, out_weight[...])
@@ -245,14 +239,12 @@
     centered = [g - mean for g in groups]
     variance = sum(jnp.sum(g * g, -1, keepdims=True) for g in centered) * (1.0 / 2048)
     inverse = lax.rsqrt(variance + 1e-05)
-    merged = jnp.concatenate(
-        [
-            (g * inverse * merge_gain[:, D * i : D * i + D]).astype(BF)
-            for i, g in enumerate(centered)
-        ],
-        1,
-    )
-    coarse = dot(merged, merge_weight[...]).astype(BF)
+    coarse = 0.0
+    for i, g in enumerate(centered):
+        part = slice(D * i, D * i + D)
+        normed = (g * inverse * merge_gain[:, part]).astype(BF)
+        coarse = coarse + dot(normed, merge_weight[part])
+    coarse = coarse.astype(BF)
     copies = []
     for r in range(2):
         for c in range(2):
@@ -266,12 +258,16 @@
                         fine[lv, 2 * a + r, f, pl.ds(c, 24, stride=2), :] = done[
                             at : at + 24, 128 * f : 128 * f + 128
                         ]
-        for a in range(3):
-            row = 2 * a + r
-            for f in range(4):
-                done_rows[:, row, :, 128 * f : 128 * f + 128] = fine[:, row, f].astype(BF)
-            copies.append(pltpu.make_async_copy(done_rows.at[:, row], out.at[:, row], sems.at[row]))
-            copies[-1].start()
+        for lv in range(2):
+            for a in range(3):
+                row = 2 * a + r
+                for f in range(4):
+                    done_rows[lv, row, :, 128 * f : 128 * f + 128] = fine[lv, row, f].astype(BF)
+                at = (lv, row)
+                copies.append(
+                    pltpu.make_async_copy(done_rows.at[at], out.at[at], sems.at[lv, row])
+                )
+                copies[-1].start()
     for copy in copies:
         copy.wait()
 
@@ -311,7 +307,8 @@
     rj = lax.ppermute(xj, "lat", cross)
 
     def edge_cells(own):
-        return jnp.concatenate([xj[:, :, own], xi[:, :, own], ri[:, :, own]], 1).reshape(144, D)
+        near = jnp.concatenate([xi[:, :, own], ri[:, :, own]], 1).reshape(96, D)
+        return jnp.concatenate([near, xj[:, :, own].reshape(48, D)], 0)
 
     first, final = slice(0, 8), slice(40, 48)
     to_left, to_right, ri = lax.optimization_barrier((edge_cells(first), edge_cells(final), ri))
@@ -319,14 +316,12 @@
     right = along(to_left, -1)
     gain = attn_gain.reshape(1, D)
 
-    scratch = [pltpu.VMEM((2, 3, 48, D), BF)]
-    qj, qi, kj, vj, oi, wi = pl.pallas_call(
+    qj, qi, kj, vj, ki, vi, kn, vn = pl.pallas_call(
         own_kernel,
         name="own_cells",
-        out_shape=[cells(F32), cells(F32), cells(BF), cells(BF), cells(F32), cells(F32)],
+        out_shape=[cells(F32)] * 2 + [cells(BF)] * 6,
         in_specs=[VMEM] * 6,
-        out_specs=[VMEM] * 6,
-        scratch_shapes=scratch * 4,
+        out_specs=[VMEM] * 8,
         compiler_params=PARAMS,
         cost_estimate=pl.CostEstimate(flops=3 * 10**9, bytes_accessed=4 * 10**6, transcendentals=10**6),
     )(xj, xi, ri, qkv_weight, gain, logit_scale.reshape(1, 8))
@@ -341,14 +336,15 @@
         far_kernel,
         name="far_rows_and_edges",
         out_shape=[chunked, flat, flat],
-        in_specs=[VMEM] * 14,
+        in_specs=[VMEM] * 16,
         out_specs=[VMEM] * 3,
         scratch_shapes=[pltpu.VMEM((2, 3, 48, D), F32)] * 2
         + [pltpu.VMEM((2, 3, 48, D), BF)] * 2
+        + [pltpu.VMEM((2, 144, D), BF)] * 2
         + [pltpu.VMEM((2, 3, 48, D), F32)],
         compiler_params=PARAMS,
-        cost_estimate=pl.CostEstimate(flops=3 * 10**9, bytes_accessed=4 * 10**6, transcendentals=10**6),
-    )(rj, left, right, xj, xi, qkv_weight, gain, out_weight, qj, qi, kj, vj, oi, wi)
+        cost_estimate=pl.CostEstimate(flops=5 * 10**8, bytes_accessed=4 * 10**6, transcendentals=10**6),
+    )(rj, left, right, xj, xi, qkv_weight, gain, out_weight, qj, qi, kj, vj, ki, vi, kn, vn)
     return pl.pallas_call(
         last_kernel,
         name="corners_merge_split",
@@ -359,7 +355,7 @@
             pltpu.VMEM((2, 6, 4, 48, 128), F32),
             pltpu.VMEM((2, 6, 4, 48, 128), F32),
             pltpu.VMEM((2, 6, 48, D), BF),
-            pltpu.SemaphoreType.DMA((6,)),
+            pltpu.SemaphoreType.DMA((2, 6)),
         ],
         compiler_params=PARAMS,
         cost_estimate=pl.CostEstimate(flops=3 * 10**9, bytes_accessed=12 * 10**6, transcendentals=10**6),

time: 24.3 us -> 23.1 us (0.951)
  the two profiles are of different devices: /device:TPU:192 before, /device:TPU:128 now
where the time goes in v3:
time: 23.1 us; the launch traced here: 22.9 us
  starting transfers between devices  11.3 us (49%)
  Pallas kernels  9.08 us (39%)
  local copies, waits for them, and re-layouts  1.25 us (5%)
  waiting for transfers between devices  1.05 us (5%)
    ppermute x4, starting transfers between devices, along(): lax.ppermute(value, 'lon', [(i, (i + steps) % count) for i in range(count)])  6.63 us
    ppermute x1, starting transfers between devices, body(): rj = lax.ppermute(xj, 'lat', cross)  4.56 us
    pallas_call x1, Pallas kernels, body(): pl.pallas_call(last_kernel, name='corners_merge_split', out_shape=jax.Sha...  3.84 us
    pallas_call x1, Pallas kernels, body(): pl.pallas_call(far_kernel, name='far_rows_and_edges', out_shape=[chunked,...  2.95 us
    pallas_call x1, Pallas kernels, body(): pl.pallas_call(own_kernel, name='own_cells', out_shape=[cells(F32)] * 2 +...  2.25 us
    unnamed x18, local copies, waits for them, and re-layouts  1.22 us
    ppermute x1, waiting for transfers between devices, body(): rj = lax.ppermute(xj, 'lat', cross)  1.03 us
  transfers between devices with their start and end apart: 6, of which 1 were waited for; matrix products, arithmetic and copies ran while one was open for 0% of the time, Pallas kernels for 23%

profile of v3, /device:TPU:128, one launch (start us, length us, event | category | flops | bytes accessed | tf_op | source)
XLA Modules:
  0.0 22.9 jit_solution(1398645872713675903)
XLA Ops:
  0.0 0.0 copy-start
  0.0 0.0 copy-start.5
  0.0 0.0 copy-start.7
  0.0 1.2 %copy-done.7 = bf16[2,6,48,512]{3,2,1,0:T(8,128)(2,1)S(1)} copy-done((bf16[2,6,48,512]{3,2,1,0:T(8,128)(2,1)S(1)}, bf16[2,6,48,512]{3,2,1,0:T(8,128)(2,1)}, u32[]{:S(2)}) %copy-start.7) | copy-done | bytes 589848
  1.2 0.0 copy-start.8
  1.2 0.1 collective-permute-start.1
  1.3 4.6 %collective-permute-start = (bf16[2,3,48,512]{3,2,1,0:T(8,128)(2,1)S(1)}, bf16[2,3,48,512]{3,2,1,0:T(8,128)(2,1)S(1)}, u32[]{:S(2)}, u32[]{:S(2)}) collective-permute-start(bf16[2,3,48,512]{3,2,1,0:T(8,128)(2,1)S(1)} %get-tuple-element.25.xj), channel_id=1, source_target_pairs={{1,2},{2,1},{3,4},{4,3},{5,6},{6,5},{7,8},{8,7},{9,10},{10,9},{11,... | collective-permute-start | bytes 884744 | tf_op jit(solution)/shard_map/ppermute | solution.py:307
  5.9 0.0 collective-permute-done.1.ri
  6.0 1.6 %collective-permute-start.4 = (bf16[144,512]{1,0:T(8,128)(2,1)S(1)}, bf16[144,512]{1,0:T(8,128)(2,1)S(1)}, u32[]{:S(2)}, u32[]{:S(2)}) collective-permute-start(bf16[144,512]{1,0:T(8,128)(2,1)S(1)} %pad_maximum_fusion.1), channel_id=1, source_target_pairs={{0,64},{64,128},{128,192},{192,0},{1,65},{65,129},{129,193},{193,1... | collective-permute-start | bytes 442376 | tf_op jit(solution)/shard_map/ppermute | solution.py:292
  7.6 1.7 %collective-permute-start.5 = (bf16[144,512]{1,0:T(8,128)(2,1)S(1)}, bf16[144,512]{1,0:T(8,128)(2,1)S(1)}, u32[]{:S(2)}, u32[]{:S(2)}) collective-permute-start(bf16[144,512]{1,0:T(8,128)(2,1)S(1)} %pad_maximum_fusion), channel_id=1, source_target_pairs={{0,192},{64,0},{128,64},{192,128},{1,193},{65,1},{129,65},{193,129... | collective-permute-start | bytes 442376 | tf_op jit(solution)/shard_map/ppermute | solution.py:292
  9.3 0.0 copy-done
  9.3 0.0 copy-done.5
  9.3 0.0 copy-done.8
  9.4 0.0 copy-start.3
  9.4 0.0 copy-start.2
  9.4 2.2 %own_cells.1 = (f32[2,3,48,512]{3,2,1,0:T(8,128)S(1)}, f32[2,3,48,512]{3,2,1,0:T(8,128)S(1)}, bf16[2,3,48,512]{3,2,1,0:T(8,128)(2,1)S(1)}, bf16[2,3,48,512]{3,2,...) custom-call(bf16[2,3,48,512]{3,2,1,0:T(8,128)(2,1)S(1)} %get-tuple-e, ...), custom_call_target="tpu_custom_call" | custom-call | flops 3000000000 | bytes 4000000 | tf_op jit(solution)/shard_map/own_cells/pallas_call | solution.py:319
  11.6 0.0 copy-start.1
  11.6 0.0 copy-start.4
  11.7 0.0 copy-start.6
  11.7 1.0 %collective-permute-done.rj = bf16[2,3,48,512]{3,2,1,0:T(8,128)(2,1)S(1)} collective-permute-done((bf16[2,3,48,512]{3,2,1,0:T(8,128)(2,1)S(1)}, bf16[2,3,48,512]{3,2,1,0:T(8,128)(2,1)S(1)}, u32[]{:S(2)}, u32[]{:S(2)}) %collective-permute-start) | collective-permute-done | bytes 294944 | tf_op jit(solution)/shard_map/ppermute | solution.py:307
  12.7 1.6 %collective-permute-start.2 = (bf16[48,512]{1,0:T(8,128)(2,1)S(1)}, bf16[48,512]{1,0:T(8,128)(2,1)S(1)}, u32[]{:S(2)}, u32[]{:S(2)}) collective-permute-start(bf16[48,512]{1,0:T(8,128)(2,1)S(1)} %bitcast.21), channel_id=1, source_target_pairs={{0,64},{64,128},{128,192},{192,0},{1,65},{65,129},{129,193},{193,1... | collective-permute-start | bytes 147464 | tf_op jit(solution)/shard_map/ppermute | solution.py:292
  14.3 1.7 %collective-permute-start.3 = (bf16[48,512]{1,0:T(8,128)(2,1)S(1)}, bf16[48,512]{1,0:T(8,128)(2,1)S(1)}, u32[]{:S(2)}, u32[]{:S(2)}) collective-permute-start(bf16[48,512]{1,0:T(8,128)(2,1)S(1)} %bitcast.20), channel_id=1, source_target_pairs={{0,192},{64,0},{128,64},{192,128},{1,193},{65,1},{129,65},{193,129... | collective-permute-start | bytes 147464 | tf_op jit(solution)/shard_map/ppermute | solution.py:292
  16.0 0.0 collective-permute-done.4.left
  16.0 0.0 collective-permute-done.5.right
  16.0 0.0 copy-done.3
  16.0 3.0 %far_rows_and_edges.1 = (f32[2,6,4,48,128]{4,3,2,1,0:T(8,128)S(1)}, f32[96,512]{1,0:T(8,128)S(1)}, f32[96,512]{1,0:T(8,128)S(1)}) custom-call(bf16[2,3,48,512]{3,2,1,0:T(8,128)(2,1)S(1)} %collective-permute-done.rj, bf16[144,512]{1,0:T(8,128)(2,1)S(1)} %collective-permute-done.4.left, bf16[144,512]{1,0:T(8,128)(2,1)S(1)} %collective-permute-done.5.right, ...), custom_call_target="tpu_custom_call" | custom-call | flops 500000000 | bytes 4000000 | tf_op jit(solution)/shard_map/far_rows_and_edges/pallas_call | solution.py:335
  19.0 0.0 collective-permute-done.2.corners_left
  19.0 0.0 collective-permute-done.3.corners_right
  19.0 0.0 copy-done.2
  19.0 0.0 copy-done.1
  19.0 0.0 copy-done.4
  19.0 0.0 copy-done.6
  19.1 3.8 %corners_merge_split.1 = bf16[2,6,48,512]{3,2,1,0:T(8,128)(2,1)} custom-call(bf16[48,512]{1,0:T(8,128)(2,1)S(1)} %collective-permute-done.2.corners_left, bf16[48,512]{1,0:T(8,128)(2,1)S(1)} %collective-permute-done.3.corners_right, bf16[2,3,48,512]{3,2,1,0:T(8,128)(2,1)S(1)} %get-tuple-element.25.xj, f32[2,3,48,512]{3,2,1,0:T(8,128)S(1)} %get-tuple-element.31.qj, ...), custom_call_target="tpu_custom_call" | custom-call | flops 3000000000 | bytes 12000000 | tf_op jit(solution)/shard_map/corners_merge_split/pallas_call | solution.py:348
  (8 shorter events, 0.1 us)
Async XLA Ops:
  0.0 9.3 %copy-start = (bf16[512,1536]{1,0:T(8,128)(2,1)S(1)}, bf16[512,1536]{1,0:T(8,128)(2,1)}, u32[]{:S(2)}) copy-start(bf16[512,1536]{1,0:T(8,128)(2,1)} %qkv.3) | copy-start | bytes 4718596
  0.0 9.3 %copy-start.5 = (f32[512]{0:T(512)S(1)}, f32[512]{0:T(512)}, u32[]{:S(2)}) copy-start(f32[512]{0:T(512)} %param.12) | copy-start | bytes 6148
  0.0 1.2 %copy-start.7 = (bf16[2,6,48,512]{3,2,1,0:T(8,128)(2,1)S(1)}, bf16[2,6,48,512]{3,2,1,0:T(8,128)(2,1)}, u32[]{:S(2)}) copy-start(bf16[2,6,48,512]{3,2,1,0:T(8,128)(2,1)} %tokens.1) | copy-start | bytes 1769476
  1.2 8.2 %copy-start.8 = (f32[8]{0:T(128)S(1)}, f32[8]{0:T(128)}, u32[]{:S(2)}) copy-start(f32[8]{0:T(128)} %param.13) | copy-start | bytes 100
  1.2 4.7 %collective-permute-start.1 = (bf16[2,3,48,512]{3,2,1,0:T(8,128)(2,1)S(1)}, bf16[2,3,48,512]{3,2,1,0:T(8,128)(2,1)S(1)}, u32[]{:S(2)}, u32[]{:S(2)}) collective-permute-start(bf16[2,3,48,512]{3,2,1,0:T(8,128)(2,1)S(1)} %get-tuple-element.26.xi), channel_id=1, source_target_pairs={{0,1},{1,0},{2,3},{3,2},{4,5},{5,4},{6,7},{7,6},{8,9},{9,8},{10,11... | collective-permute-start | bytes 884744 | tf_op jit(solution)/shard_map/ppermute | solution.py:306
  1.3 11.4 %collective-permute-start = (bf16[2,3,48,512]{3,2,1,0:T(8,128)(2,1)S(1)}, bf16[2,3,48,512]{3,2,1,0:T(8,128)(2,1)S(1)}, u32[]{:S(2)}, u32[]{:S(2)}) collective-permute-start(bf16[2,3,48,512]{3,2,1,0:T(8,128)(2,1)S(1)} %get-tuple-element.25.xj), channel_id=1, source_target_pairs={{1,2},{2,1},{3,4},{4,3},{5,6},{6,5},{7,8},{8,7},{9,10},{10,9},{11,... | collective-permute-start | bytes 884744 | tf_op jit(solution)/shard_map/ppermute | solution.py:307
  6.0 10.0 %collective-permute-start.4 = (bf16[144,512]{1,0:T(8,128)(2,1)S(1)}, bf16[144,512]{1,0:T(8,128)(2,1)S(1)}, u32[]{:S(2)}, u32[]{:S(2)}) collective-permute-start(bf16[144,512]{1,0:T(8,128)(2,1)S(1)} %pad_maximum_fusion.1), channel_id=1, source_target_pairs={{0,64},{64,128},{128,192},{192,0},{1,65},{65,129},{129,193},{193,1... | collective-permute-start | bytes 442376 | tf_op jit(solution)/shard_map/ppermute | solution.py:292
  7.6 8.4 %collective-permute-start.5 = (bf16[144,512]{1,0:T(8,128)(2,1)S(1)}, bf16[144,512]{1,0:T(8,128)(2,1)S(1)}, u32[]{:S(2)}, u32[]{:S(2)}) collective-permute-start(bf16[144,512]{1,0:T(8,128)(2,1)S(1)} %pad_maximum_fusion), channel_id=1, source_target_pairs={{0,192},{64,0},{128,64},{192,128},{1,193},{65,1},{129,65},{193,129... | collective-permute-start | bytes 442376 | tf_op jit(solution)/shard_map/ppermute | solution.py:292
  9.4 6.7 %copy-start.3 = (bf16[512,512]{1,0:T(8,128)(2,1)S(1)}, bf16[512,512]{1,0:T(8,128)(2,1)}, u32[]{:S(2)}) copy-start(bf16[512,512]{1,0:T(8,128)(2,1)} %out_weight.3) | copy-start | bytes 1572868
  9.4 9.7 %copy-start.2 = (bf16[1024,2048]{1,0:T(8,128)(2,1)S(1)}, bf16[1024,2048]{1,0:T(8,128)(2,1)}, u32[]{:S(2)}) copy-start(bf16[1024,2048]{1,0:T(8,128)(2,1)} %split_weight.1) | copy-start | bytes 12582916
  11.6 7.4 %copy-start.1 = (bf16[2048,1024]{1,0:T(8,128)(2,1)S(1)}, bf16[2048,1024]{1,0:T(8,128)(2,1)}, u32[]{:S(2)}) copy-start(bf16[2048,1024]{1,0:T(8,128)(2,1)} %merge_weight.1) | copy-start | bytes 12582916
  11.6 7.4 %copy-start.4 = (f32[2048]{0:T(1024)S(1)}, f32[2048]{0:T(1024)}, u32[]{:S(2)}) copy-start(f32[2048]{0:T(1024)} %param.15) | copy-start | bytes 24580
  11.7 7.4 %copy-start.6 = (f32[512]{0:T(512)S(1)}, f32[512]{0:T(512)}, u32[]{:S(2)}) copy-start(f32[512]{0:T(512)} %param.17) | copy-start | bytes 6148
  12.7 6.3 %collective-permute-start.2 = (bf16[48,512]{1,0:T(8,128)(2,1)S(1)}, bf16[48,512]{1,0:T(8,128)(2,1)S(1)}, u32[]{:S(2)}, u32[]{:S(2)}) collective-permute-start(bf16[48,512]{1,0:T(8,128)(2,1)S(1)} %bitcast.21), channel_id=1, source_target_pairs={{0,64},{64,128},{128,192},{192,0},{1,65},{65,129},{129,193},{193,1... | collective-permute-start | bytes 147464 | tf_op jit(solution)/shard_map/ppermute | solution.py:292
  14.3 4.7 %collective-permute-start.3 = (bf16[48,512]{1,0:T(8,128)(2,1)S(1)}, bf16[48,512]{1,0:T(8,128)(2,1)S(1)}, u32[]{:S(2)}, u32[]{:S(2)}) collective-permute-start(bf16[48,512]{1,0:T(8,128)(2,1)S(1)} %bitcast.20), channel_id=1, source_target_pairs={{0,192},{64,0},{128,64},{192,128},{1,193},{65,1},{129,65},{193,129... | collective-permute-start | bytes 147464 | tf_op jit(solution)/shard_map/ppermute | solution.py:292

commit v4 on v3

--- a/solution.py
+++ b/solution.py
@@ -69,33 +69,30 @@
     return jnp.where((lat > 0) & (lat < lax.axis_size("lat") - 1), 1.0, 0.0)
 
 
-def window_mask(ch, lv, near, present):
+def window_mask(ch):
     query = lax.broadcasted_iota(jnp.int32, (72, 240), 0)
     key = lax.broadcasted_iota(jnp.int32, (72, 240), 1)
     row = (query >= 24).astype(jnp.int32) + (query >= 48).astype(jnp.int32)
-    edge = key >= 192
-    column = jnp.where(edge, (48 if ch else -8) + (key & 7), 16 * ch + (key & 31))
+    column = jnp.where(key >= 192, (48 if ch else -8) + (key & 7), 16 * ch + (key & 31))
     same = window(24 * ch + query - 24 * row) == window(column)
-    if near:
-        value = jnp.where(same, 1.0, 0.0)
-    else:
-        other = (key >= 96) & (key < 192)
-        level = (key < 216) if lv == 0 else (key < 192) | (key >= 216)
-        value = jnp.where(same & level, jnp.where(other, present, 1.0), 0.0)
-    return jnp.concatenate([value] * 4, 0)
+    return jnp.where(same, 1.0, 0.0)
+
+
+def far_keys(lv, present):
+    key = lax.broadcasted_iota(jnp.int32, (1, 240), 1)
+    level = (key < 216) if lv == 0 else (key < 192) | (key >= 216)
+    other = (key >= 96) & (key < 192)
+    return jnp.where(level, jnp.where(other, present, 1.0), 0.0)
 
 
 def corner_mask(present):
     query = lax.broadcasted_iota(jnp.int32, (96, 96), 0)
     key = lax.broadcasted_iota(jnp.int32, (96, 96), 1)
-    keep = query < 0
-    for group in range(4):
-        side = group // 2
-        rows = (query >= 24 * group) & (query < 24 * group + 24)
-        keys = (key >= 24 * group) & (key < 24 * group + 24)
-        same = window(40 * side + (query & 7)) == window((48 if side else -8) + (key & 7))
-        keep = keep | (rows & keys & same)
-    return jnp.concatenate([jnp.where(keep, present, 0.0)] * 4, 0)
+    group = lax.shift_right_logical(query * 2731, 16) == lax.shift_right_logical(key * 2731, 16)
+    query = jnp.where(query >= 48, 40, 0) + (query & 7)
+    key = jnp.where(key >= 48, 48, -8) + (key & 7)
+    same = window(query) == window(key)
+    return jnp.concatenate([jnp.where(same & group, present, 0.0)] * 4, 0)
 
 
 def head_blocks():
@@ -107,8 +104,10 @@
 
 def attend_half(q, kown, vown, kpart, vpart, kedge, vedge, near, present, store):
     for ch in range(2):
+        base = window_mask(ch)
         for lv in range(2):
-            mask = window_mask(ch, lv, near, present)
+            mask = base if near else base * far_keys(lv, present)
+            mask = jnp.concatenate([mask] * 4, 0)
             qs = jnp.concatenate([q[lv, r, 24 * ch : 24 * ch + 24] for r in range(3)], 0)
             cells = slice(16 * ch, 16 * ch + 32)
             edge = slice(48 * lv, 48 * lv + 48) if near else slice(96, 144)
@@ -129,28 +128,39 @@
     return dot(normed, weight[:, columns])
 
 
-def rows_kernel(tokens, near, far):
+def rows_kernel(tokens, far, near):
     start = 3 * lax.rem(lax.axis_index("lat"), 2)
     near[...] = tokens[:, pl.ds(3 - start, 3)]
     far[...] = tokens[:, pl.ds(start, 3)]
 
 
-def own_kernel(xj, xi, ri, weight, gain, scales, qj, qi, kj, vj, ki, vi, kr, vr):
-    block = head_blocks()
+def head_scale(scales):
     lane = lax.broadcasted_iota(jnp.int32, (1, D), 1)
     scale = jnp.zeros((1, D), F32)
     for h in range(8):
         scale = jnp.where(lax.shift_right_logical(lane, 6) == h, scales[:, h : h + 1], scale)
-    scale = scale * LOG2E
+    return scale * LOG2E
+
+
+def own_half(x, weight, gain, scale, block, q, k, v):
     for lv in range(2):
-        for x, q, k, v in ((xi, qi, ki, vi), (xj, qj, kj, vj)):
-            all3 = project(x, lv, gain[...], weight, slice(0, 1536))
-            q[lv] = head_scaled(all3[:, :D], block, scale).reshape(3, 48, D)
-            k[lv] = head_scaled(all3[:, D : 2 * D], block).astype(BF).reshape(3, 48, D)
-            v[lv] = all3[:, 2 * D :].astype(BF).reshape(3, 48, D)
-        both = project(ri, lv, gain[...], weight, slice(512, 1536))
-        kr[lv] = head_scaled(both[:, :D], block).astype(BF).reshape(3, 48, D)
-        vr[lv] = both[:, D:].astype(BF).reshape(3, 48, D)
+        all3 = project(x, lv, gain, weight, slice(0, 1536))
+        q[lv] = head_scaled(all3[:, :D], block, scale).reshape(3, 48, D)
+        k[lv] = head_scaled(all3[:, D : 2 * D], block).astype(BF).reshape(3, 48, D)
+        v[lv] = all3[:, 2 * D :].astype(BF).reshape(3, 48, D)
+
+
+def own_kernel(xj, weight, gain, scales, qj, kj, vj):
+    own_half(xj, weight, gain[...], head_scale(scales), head_blocks(), qj, kj, vj)
+
+
+def near_kernel(xi, ri, weight, gain, scales, qi, ki, vi, kr, vr):
+    block = head_blocks()
+    own_half(xi, weight, gain[...], head_scale(scales), block, qi, ki, vi)
+    for lv in range(2):
+        k, v = keys_values(ri[lv].reshape(144, D), weight, gain[...], block)
+        kr[lv] = k.reshape(3, 48, D)
+        vr[lv] = v.reshape(3, 48, D)
 
 
 def keys_values(tokens, qkv, gain, block):
@@ -294,7 +304,7 @@
     def cells(dtype):
         return jax.ShapeDtypeStruct((2, 3, 48, D), dtype)
 
-    xi, xj = pl.pallas_call(
+    xj, xi = pl.pallas_call(
         rows_kernel,
         name="rows",
         out_shape=[cells(BF), cells(BF)],
@@ -316,17 +326,27 @@
     right = along(to_left, -1)
     gain = attn_gain.reshape(1, D)
 
-    qj, qi, kj, vj, ki, vi, kn, vn = pl.pallas_call(
+    scales = logit_scale.reshape(1, 8)
+    qj, kj, vj = pl.pallas_call(
         own_kernel,
-        name="own_cells",
-        out_shape=[cells(F32)] * 2 + [cells(BF)] * 6,
-        in_specs=[VMEM] * 6,
-        out_specs=[VMEM] * 8,
+        name="own_far_rows",
+        out_shape=[cells(F32)] + [cells(BF)] * 2,
+        in_specs=[VMEM] * 4,
+        out_specs=[VMEM] * 3,
         compiler_params=PARAMS,
         cost_estimate=pl.CostEstimate(flops=3 * 10**9, bytes_accessed=4 * 10**6, transcendentals=10**6),
-    )(xj, xi, ri, qkv_weight, gain, logit_scale.reshape(1, 8))
-    corner_left, corner_right, rj, qj = lax.optimization_barrier(
-        (rj[:, :, first].reshape(48, D), rj[:, :, final].reshape(48, D), rj, qj)
+    )(xj, qkv_weight, gain, scales)
+    qi, ki, vi, kn, vn = pl.pallas_call(
+        near_kernel,
+        name="near_rows",
+        out_shape=[cells(F32)] + [cells(BF)] * 4,
+        in_specs=[VMEM] * 5,
+        out_specs=[VMEM] * 5,
+        compiler_params=PARAMS,
+        cost_estimate=pl.CostEstimate(flops=10**7, bytes_accessed=2 * 10**6, transcendentals=10**5),
+    )(xi, ri, qkv_weight, gain, scales)
+    corner_left, corner_right, rj, qj, kn = lax.optimization_barrier(
+        (rj[:, :, first].reshape(48, D), rj[:, :, final].reshape(48, D), rj, qj, kn)
     )
     corners_left = along(corner_right, 1)
     corners_right = along(corner_left, -1)

time: 23.1 us -> 23 us (level)
  starting transfers between devices: 11.3 us -> 10.6 us
  waiting for transfers between devices: 1.05 us -> 1.39 us
    ppermute x1, starting transfers between devices: 4.56 us -> 3.91 us  [body(): rj = lax.ppermute(xj, 'lat', cross)]
    ppermute x1, waiting for transfers between devices: 0.01 us -> 0.5 us  [body(): ri = lax.ppermute(xi, 'lat', pair)]
    pallas_call x1 -> x2, Pallas kernels: 2.25 us -> 2.43 us  [the longest x1 1.44 us: body(): pl.pallas_call(near_kernel, name='near_rows', out_shape=[cells(F32)] + [c...]
  transfers between devices with their start and end apart: 6 -> 6, of which waited for: 1 -> 2; matrix products, arithmetic and copies ran while one was open for 0% -> 0% of each run, Pallas kernels for 23% -> 24%
where the time goes in v4:
time: 23 us; the launch traced here: 22.8 us
  starting transfers between devices  10.6 us (46%)
  Pallas kernels  9.28 us (40%)
  waiting for transfers between devices  1.39 us (6%)
  local copies, waits for them, and re-layouts  1.25 us (5%)
    ppermute x4, starting transfers between devices, along(): lax.ppermute(value, 'lon', [(i, (i + steps) % count) for i in range(count)])  6.63 us
    ppermute x1, starting transfers between devices, body(): rj = lax.ppermute(xj, 'lat', cross)  3.91 us
    pallas_call x1, Pallas kernels, body(): pl.pallas_call(last_kernel, name='corners_merge_split', out_shape=jax.Sha...  3.84 us
    pallas_call x1, Pallas kernels, body(): pl.pallas_call(far_kernel, name='far_rows_and_edges', out_shape=[chunked,...  2.97 us
    pallas_call x1, Pallas kernels, body(): pl.pallas_call(near_kernel, name='near_rows', out_shape=[cells(F32)] + [c...  1.44 us
    unnamed x18, local copies, waits for them, and re-layouts  1.22 us
    pallas_call x1, Pallas kernels, body(): pl.pallas_call(own_kernel, name='own_far_rows', out_shape=[cells(F32)] +...  0.99 us
    ppermute x1, waiting for transfers between devices, body(): rj = lax.ppermute(xj, 'lat', cross)  0.87 us
  transfers between devices with their start and end apart: 6, of which 2 were waited for; matrix products, arithmetic and copies ran while one was open for 0% of the time, Pallas kernels for 24%

profile of v4, /device:TPU:128, one launch (start us, length us, event | category | flops | bytes accessed | tf_op | source)
XLA Modules:
  0.0 22.8 jit_solution(16597402834750280163)
XLA Ops:
  0.0 0.0 copy-start
  0.0 0.0 copy-start.4
  0.0 0.0 copy-start.7
  0.0 0.0 copy-start.8
  0.0 1.2 %copy-done.8 = bf16[2,6,48,512]{3,2,1,0:T(8,128)(2,1)S(1)} copy-done((bf16[2,6,48,512]{3,2,1,0:T(8,128)(2,1)S(1)}, bf16[2,6,48,512]{3,2,1,0:T(8,128)(2,1)}, u32[]{:S(2)}) %copy-start.8) | copy-done | bytes 589848
  1.2 3.9 %collective-permute-start = (bf16[2,3,48,512]{3,2,1,0:T(8,128)(2,1)S(1)}, bf16[2,3,48,512]{3,2,1,0:T(8,128)(2,1)S(1)}, u32[]{:S(2)}, u32[]{:S(2)}) collective-permute-start(bf16[2,3,48,512]{3,2,1,0:T(8,128)(2,1)S(1)} %get-tuple-element.26.xj), channel_id=1, source_target_pairs={{1,2},{2,1},{3,4},{4,3},{5,6},{6,5},{7,8},{8,7},{9,10},{10,9},{11,... | collective-permute-start | bytes 884744 | tf_op jit(solution)/shard_map/ppermute | solution.py:317
  5.2 0.1 collective-permute-start.1
  5.3 0.0 copy-done
  5.3 0.0 copy-done.4
  5.3 0.0 copy-done.7
  5.3 0.0 copy-start.3
  5.3 1.0 %own_far_rows.1 = (f32[2,3,48,512]{3,2,1,0:T(8,128)S(1)}, bf16[2,3,48,512]{3,2,1,0:T(8,128)(2,1)S(1)}, bf16[2,3,48,512]{3,2,1,0:T(8,128)(2,1)S(1)}) custom-call(bf16[2,3,48,512]{3,2,1,0:T(8,128)(2,1)S(1)} %get-tuple-element.26.xj, bf16[512,1536]{1,0:T(8,128)(2,1)S(1)} %copy-done, f32[1,512]{1,0:T(1,128)S(1)} %bitcast.10, f32[1,8]{1,0:T(1,128)S(1)} %bitcast.16), custom_call_target="tpu_custom_call" | custom-call | flops 3000000000 | bytes 4000000 | tf_op jit(solution)/shard_map/own_far_rows/pallas_call | solution.py:330
  6.3 0.5 %collective-permute-done.1.ri = bf16[2,3,48,512]{3,2,1,0:T(8,128)(2,1)S(1)} collective-permute-done((bf16[2,3,48,512]{3,2,1,0:T(8,128)(2,1)S(1)}, bf16[2,3,48,512]{3,2,1,0:T(8,128)(2,1)S(1)}, u32[]{:S(2)}, u32[]{:S(2)}) %collective-permute-start.1) | collective-permute-done | bytes 294944 | tf_op jit(solution)/shard_map/ppermute | solution.py:316
  6.9 0.0 copy-start.1
  6.9 0.0 copy-start.2
  6.9 0.0 copy-start.5
  6.9 0.0 copy-start.6
  7.0 1.6 %collective-permute-start.4 = (bf16[144,512]{1,0:T(8,128)(2,1)S(1)}, bf16[144,512]{1,0:T(8,128)(2,1)S(1)}, u32[]{:S(2)}, u32[]{:S(2)}) collective-permute-start(bf16[144,512]{1,0:T(8,128)(2,1)S(1)} %pad_maximum_fusion.1), channel_id=1, source_target_pairs={{0,64},{64,128},{128,192},{192,0},{1,65},{65,129},{129,193},{193,1... | collective-permute-start | bytes 442376 | tf_op jit(solution)/shard_map/ppermute | solution.py:302
  8.5 1.7 %collective-permute-start.5 = (bf16[144,512]{1,0:T(8,128)(2,1)S(1)}, bf16[144,512]{1,0:T(8,128)(2,1)S(1)}, u32[]{:S(2)}, u32[]{:S(2)}) collective-permute-start(bf16[144,512]{1,0:T(8,128)(2,1)S(1)} %pad_maximum_fusion), channel_id=1, source_target_pairs={{0,192},{64,0},{128,64},{192,128},{1,193},{65,1},{129,65},{193,129... | collective-permute-start | bytes 442376 | tf_op jit(solution)/shard_map/ppermute | solution.py:302
  10.3 1.4 %near_rows.1 = (f32[2,3,48,512]{3,2,1,0:T(8,128)S(1)}, bf16[2,3,48,512]{3,2,1,0:T(8,128)(2,1)S(1)}, bf16[2,3,48,512]{3,2,1,0:T(8,128)(2,1)S(1)}, bf16[2,3,48,512...) custom-call(bf16[2,3,48,512]{3,2,1,0:T(8,128)(2,1)S(1)} %get-tuple-element.28.xi, ...), custom_call_target="tpu_custom_call" | custom-call | flops 10000000 | bytes 2000000 | tf_op jit(solution)/shard_map/near_rows/pallas_call | solution.py:339
  11.7 0.9 %collective-permute-done.rj = bf16[2,3,48,512]{3,2,1,0:T(8,128)(2,1)S(1)} collective-permute-done((bf16[2,3,48,512]{3,2,1,0:T(8,128)(2,1)S(1)}, bf16[2,3,48,512]{3,2,1,0:T(8,128)(2,1)S(1)}, u32[]{:S(2)}, u32[]{:S(2)}) %collective-permute-start) | collective-permute-done | bytes 294944 | tf_op jit(solution)/shard_map/ppermute | solution.py:317
  12.6 1.6 %collective-permute-start.2 = (bf16[48,512]{1,0:T(8,128)(2,1)S(1)}, bf16[48,512]{1,0:T(8,128)(2,1)S(1)}, u32[]{:S(2)}, u32[]{:S(2)}) collective-permute-start(bf16[48,512]{1,0:T(8,128)(2,1)S(1)} %bitcast.23), channel_id=1, source_target_pairs={{0,64},{64,128},{128,192},{192,0},{1,65},{65,129},{129,193},{193,1... | collective-permute-start | bytes 147464 | tf_op jit(solution)/shard_map/ppermute | solution.py:302
  14.2 1.7 %collective-permute-start.3 = (bf16[48,512]{1,0:T(8,128)(2,1)S(1)}, bf16[48,512]{1,0:T(8,128)(2,1)S(1)}, u32[]{:S(2)}, u32[]{:S(2)}) collective-permute-start(bf16[48,512]{1,0:T(8,128)(2,1)S(1)} %bitcast.22), channel_id=1, source_target_pairs={{0,192},{64,0},{128,64},{192,128},{1,193},{65,1},{129,65},{193,129... | collective-permute-start | bytes 147464 | tf_op jit(solution)/shard_map/ppermute | solution.py:302
  15.9 0.0 collective-permute-done.4.left
  15.9 0.0 collective-permute-done.5.right
  15.9 0.0 copy-done.3
  15.9 3.0 %far_rows_and_edges.1 = (f32[2,6,4,48,128]{4,3,2,1,0:T(8,128)S(1)}, f32[96,512]{1,0:T(8,128)S(1)}, f32[96,512]{1,0:T(8,128)S(1)}) custom-call(bf16[2,3,48,512]{3,2,1,0:T(8,128)(2,1)S(1)} %collective-permute-done.rj, bf16[144,512]{1,0:T(8,128)(2,1)S(1)} %collective-permute-done.4.left, bf16[144,512]{1,0:T(8,128)(2,1)S(1)} %collective-permute-done.5.right, ...), custom_call_target="tpu_custom_call" | custom-call | flops 500000000 | bytes 4000000 | tf_op jit(solution)/shard_map/far_rows_and_edges/pallas_call | solution.py:355
  18.9 0.0 collective-permute-done.2.corners_left
  18.9 0.0 collective-permute-done.3.corners_right
  18.9 0.0 copy-done.1
  18.9 0.0 copy-done.2
  19.0 0.0 copy-done.5
  19.0 0.0 copy-done.6
  19.0 3.8 %corners_merge_split.1 = bf16[2,6,48,512]{3,2,1,0:T(8,128)(2,1)} custom-call(bf16[48,512]{1,0:T(8,128)(2,1)S(1)} %collective-permute-done.2.corners_left, bf16[48,512]{1,0:T(8,128)(2,1)S(1)} %collective-permute-done.3.corners_right, bf16[2,3,48,512]{3,2,1,0:T(8,128)(2,1)S(1)} %get-tuple-element.26.xj, f32[2,3,48,512]{3,2,1,0:T(8,128)S(1)} %get-tuple-element.33.qj, ...), custom_call_target="tpu_custom_call" | custom-call | flops 3000000000 | bytes 12000000 | tf_op jit(solution)/shard_map/corners_merge_split/pallas_call | solution.py:368
  (8 shorter events, 0.1 us)
Async XLA Ops:
  0.0 5.3 %copy-start = (bf16[512,1536]{1,0:T(8,128)(2,1)S(1)}, bf16[512,1536]{1,0:T(8,128)(2,1)}, u32[]{:S(2)}) copy-start(bf16[512,1536]{1,0:T(8,128)(2,1)} %qkv.3) | copy-start | bytes 4718596
  0.0 5.3 %copy-start.4 = (f32[512]{0:T(512)S(1)}, f32[512]{0:T(512)}, u32[]{:S(2)}) copy-start(f32[512]{0:T(512)} %param.12) | copy-start | bytes 6148
  0.0 5.3 %copy-start.7 = (f32[8]{0:T(128)S(1)}, f32[8]{0:T(128)}, u32[]{:S(2)}) copy-start(f32[8]{0:T(128)} %param.13) | copy-start | bytes 100
  0.0 1.2 %copy-start.8 = (bf16[2,6,48,512]{3,2,1,0:T(8,128)(2,1)S(1)}, bf16[2,6,48,512]{3,2,1,0:T(8,128)(2,1)}, u32[]{:S(2)}) copy-start(bf16[2,6,48,512]{3,2,1,0:T(8,128)(2,1)} %tokens.1) | copy-start | bytes 1769476
  1.2 11.4 %collective-permute-start = (bf16[2,3,48,512]{3,2,1,0:T(8,128)(2,1)S(1)}, bf16[2,3,48,512]{3,2,1,0:T(8,128)(2,1)S(1)}, u32[]{:S(2)}, u32[]{:S(2)}) collective-permute-start(bf16[2,3,48,512]{3,2,1,0:T(8,128)(2,1)S(1)} %get-tuple-element.26.xj), channel_id=1, source_target_pairs={{1,2},{2,1},{3,4},{4,3},{5,6},{6,5},{7,8},{8,7},{9,10},{10,9},{11,... | collective-permute-start | bytes 884744 | tf_op jit(solution)/shard_map/ppermute | solution.py:317
  5.2 1.7 %collective-permute-start.1 = (bf16[2,3,48,512]{3,2,1,0:T(8,128)(2,1)S(1)}, bf16[2,3,48,512]{3,2,1,0:T(8,128)(2,1)S(1)}, u32[]{:S(2)}, u32[]{:S(2)}) collective-permute-start(bf16[2,3,48,512]{3,2,1,0:T(8,128)(2,1)S(1)} %get-tuple-element.28.xi), channel_id=1, source_target_pairs={{0,1},{1,0},{2,3},{3,2},{4,5},{5,4},{6,7},{7,6},{8,9},{9,8},{10,11... | collective-permute-start | bytes 884744 | tf_op jit(solution)/shard_map/ppermute | solution.py:316
  5.3 10.6 %copy-start.3 = (bf16[512,512]{1,0:T(8,128)(2,1)S(1)}, bf16[512,512]{1,0:T(8,128)(2,1)}, u32[]{:S(2)}) copy-start(bf16[512,512]{1,0:T(8,128)(2,1)} %out_weight.3) | copy-start | bytes 1572868
  6.9 12.0 %copy-start.1 = (bf16[2048,1024]{1,0:T(8,128)(2,1)S(1)}, bf16[2048,1024]{1,0:T(8,128)(2,1)}, u32[]{:S(2)}) copy-start(bf16[2048,1024]{1,0:T(8,128)(2,1)} %merge_weight.1) | copy-start | bytes 12582916
  6.9 12.0 %copy-start.2 = (bf16[1024,2048]{1,0:T(8,128)(2,1)S(1)}, bf16[1024,2048]{1,0:T(8,128)(2,1)}, u32[]{:S(2)}) copy-start(bf16[1024,2048]{1,0:T(8,128)(2,1)} %split_weight.1) | copy-start | bytes 12582916
  6.9 12.0 %copy-start.5 = (f32[2048]{0:T(1024)S(1)}, f32[2048]{0:T(1024)}, u32[]{:S(2)}) copy-start(f32[2048]{0:T(1024)} %param.15) | copy-start | bytes 24580
  6.9 12.0 %copy-start.6 = (f32[512]{0:T(512)S(1)}, f32[512]{0:T(512)}, u32[]{:S(2)}) copy-start(f32[512]{0:T(512)} %param.17) | copy-start | bytes 6148
  7.0 9.0 %collective-permute-start.4 = (bf16[144,512]{1,0:T(8,128)(2,1)S(1)}, bf16[144,512]{1,0:T(8,128)(2,1)S(1)}, u32[]{:S(2)}, u32[]{:S(2)}) collective-permute-start(bf16[144,512]{1,0:T(8,128)(2,1)S(1)} %pad_maximum_fusion.1), channel_id=1, source_target_pairs={{0,64},{64,128},{128,192},{192,0},{1,65},{65,129},{129,193},{193,1... | collective-permute-start | bytes 442376 | tf_op jit(solution)/shard_map/ppermute | solution.py:302
  8.5 7.4 %collective-permute-start.5 = (bf16[144,512]{1,0:T(8,128)(2,1)S(1)}, bf16[144,512]{1,0:T(8,128)(2,1)S(1)}, u32[]{:S(2)}, u32[]{:S(2)}) collective-permute-start(bf16[144,512]{1,0:T(8,128)(2,1)S(1)} %pad_maximum_fusion), channel_id=1, source_target_pairs={{0,192},{64,0},{128,64},{192,128},{1,193},{65,1},{129,65},{193,129... | collective-permute-start | bytes 442376 | tf_op jit(solution)/shard_map/ppermute | solution.py:302
  12.6 6.3 %collective-permute-start.2 = (bf16[48,512]{1,0:T(8,128)(2,1)S(1)}, bf16[48,512]{1,0:T(8,128)(2,1)S(1)}, u32[]{:S(2)}, u32[]{:S(2)}) collective-permute-start(bf16[48,512]{1,0:T(8,128)(2,1)S(1)} %bitcast.23), channel_id=1, source_target_pairs={{0,64},{64,128},{128,192},{192,0},{1,65},{65,129},{129,193},{193,1... | collective-permute-start | bytes 147464 | tf_op jit(solution)/shard_map/ppermute | solution.py:302
  14.2 4.7 %collective-permute-start.3 = (bf16[48,512]{1,0:T(8,128)(2,1)S(1)}, bf16[48,512]{1,0:T(8,128)(2,1)S(1)}, u32[]{:S(2)}, u32[]{:S(2)}) collective-permute-start(bf16[48,512]{1,0:T(8,128)(2,1)S(1)} %bitcast.22), channel_id=1, source_target_pairs={{0,192},{64,0},{128,64},{192,128},{1,193},{65,1},{129,65},{193,129... | collective-permute-start | bytes 147464 | tf_op jit(solution)/shard_map/ppermute | solution.py:302
